TPU v7x, 128 devices: a whole 4x4x4 slice. The times are simulated.
128 devices in a mesh: tx: 8 (over x, y_hi), ty: 16 (over z, y_lo, core).
Axes of the slice: x: 4, y: 4 (y_hi: 2, y_lo: 2; y = y_hi * 2 + y_lo), z: 4, core: 2. Of those that a mesh axis runs over, the one named last changes fastest.
Arguments:
- seed_fluid: float32 [64, 512, 1024], P('ty', 'tx'), may hold values from -6 to 6
- seed_plate: float32 [16, 512, 1024], P(None, 'ty', 'tx'), may hold values from -6 to 6
- velocity: bfloat16 [4, 3, 64, 512, 1024], P(None, None, 'ty', 'tx'), may hold values from -4 to 4
- enthalpy: float32 [4, 16, 512, 1024], P(None, None, 'ty', 'tx'), may hold values from 0 to 1
- phase: int32 [4, 16, 512, 1024], P(None, None, 'ty', 'tx'), may hold values from 0 to 2
- contact: int32 [512, 1024], P('ty', 'tx'), may hold values 0 or 1
Outputs:
- adjoint_fluid: float32 [64, 512, 1024], P('ty', 'tx')
- adjoint_plate: float32 [16, 512, 1024], P(None, 'ty', 'tx')
All inputs are finite; a program needn't handle non-finite values. No bound on the sum of `contact` on one device may be relied on, other than what follows from the above.
Results may differ from a plain program's by a relative error of at most 0.0003.
Values sent between devices are 32-bit elements; how exact they have to be, the bound alone decides.
A program may use at most 128 MiB of HBM per device.

v0:
```python
import jax
import jax.numpy as jnp
from jax import lax
from jax.sharding import PartitionSpec as P

STEPS = 4


DIFFUSION = 0.1
ADVECTION = 0.2
PLATE_DIFFUSION = 0.12
FLUID_COUPLING = 0.5
PLATE_COUPLING = 0.5


def with_halo(block, sides, width):
    for axis, dim in sides:
        count = lax.axis_size(axis)
        forward = [(i, i + 1) for i in range(count - 1)]
        backward = [(target, source) for source, target in forward]
        low = lax.ppermute(
            lax.slice_in_dim(block, block.shape[dim] - width, None, axis=dim), axis, forward
        )
        high = lax.ppermute(lax.slice_in_dim(block, 0, width, axis=dim), axis, backward)
        block = jnp.concatenate([low, block, high], axis=dim)
    return block


def phase_slopes(states, saved):
    mushy = 1.0 / (1.0 + 8.0 * saved * (1.0 - saved))
    return jnp.where(states == 0, 1.0, jnp.where(states == 2, 0.7, mushy))


def to_plate(wall_layer, is_owner):
    spread = lax.all_to_all(wall_layer, "tx", split_axis=1, concat_axis=0, tiled=True)
    return lax.psum_scatter(jnp.where(is_owner, spread, 0.0), "ty", scatter_dimension=0, tiled=True)


def fluid_terms(adjoint_fluid, speed_y, speed_z):
    stacked = jnp.stack([adjoint_fluid, speed_y * adjoint_fluid, speed_z * adjoint_fluid])
    padded = with_halo(stacked, (("tx", 2), ("ty", 1)), 1)
    center = padded[0]
    lateral = center[2:, 1:-1] + center[:-2, 1:-1] + center[1:-1, 2:] + center[1:-1, :-2]
    moved = 0.5 * (padded[1][1:-1, 2:] - padded[1][1:-1, :-2])
    moved = moved + 0.5 * (padded[2][2:, 1:-1] - padded[2][:-2, 1:-1])
    return (lateral, moved)


def on_device(seed_fluid, seed_plate, velocity, enthalpy, phase, contact):
    adjoint_fluid = seed_fluid
    adjoint_plate = seed_plate
    contact_map = contact.astype(jnp.float32)
    is_owner = lax.axis_index("ty") == 0
    for step in reversed(range(STEPS)):
        speed_x = velocity[step, 0].astype(jnp.float32)
        speed_y = velocity[step, 1].astype(jnp.float32)
        speed_z = velocity[step, 2].astype(jnp.float32)
        lateral, moved = fluid_terms(adjoint_fluid, speed_y, speed_z)
        along_x = jnp.pad(adjoint_fluid, ((0, 0), (0, 0), (1, 1)))
        flux_x = jnp.pad(speed_x * adjoint_fluid, ((0, 0), (0, 0), (1, 1)))
        fluid_lap = lateral + along_x[:, :, 2:] + along_x[:, :, :-2] - 6.0 * adjoint_fluid
        advected = 0.5 * (flux_x[:, :, 2:] - flux_x[:, :, :-2]) + moved
        plate_wall = to_plate(adjoint_fluid[0], is_owner)
        coupling = contact_map * (PLATE_COUPLING * adjoint_plate[-1] - FLUID_COUPLING * plate_wall)
        returned = lax.all_gather(coupling, "ty", axis=0, tiled=True)
        returned = lax.all_to_all(returned, "tx", split_axis=0, concat_axis=1, tiled=True)
        fluid_next = adjoint_fluid + DIFFUSION * fluid_lap + ADVECTION * advected
        fluid_next = fluid_next.at[0].add(jnp.where(is_owner, returned, 0.0))
        plate_halo = with_halo(adjoint_plate, (("tx", 2), ("ty", 1)), 1)
        along_z = jnp.pad(adjoint_plate, ((1, 1), (0, 0), (0, 0)))
        plate_lap = (
            plate_halo[:, 2:, 1:-1]
            + plate_halo[:, :-2, 1:-1]
            + plate_halo[:, 1:-1, 2:]
            + plate_halo[:, 1:-1, :-2]
        )
        plate_lap = plate_lap + along_z[2:] + along_z[:-2] - 6.0 * adjoint_plate
        forcing = PLATE_DIFFUSION * plate_lap
        forcing = forcing.at[-1].add(-coupling)
        slopes = phase_slopes(phase[step], enthalpy[step])
        adjoint_plate = adjoint_plate + slopes * forcing
        adjoint_fluid = fluid_next
    return (adjoint_fluid, adjoint_plate)


def solution(mesh):
    return jax.shard_map(
        on_device,
        mesh=mesh,
        in_specs=(
            P("ty", "tx", None),
            P(None, "ty", "tx"),
            P(None, None, "ty", "tx", None),
            P(None, None, "ty", "tx"),
            P(None, None, "ty", "tx"),
            P("ty", "tx"),
        ),
        out_specs=(P("ty", "tx", None), P(None, "ty", "tx")),
        check_vma=False,
    )
```

profile of v0, /device:TPU:6, one launch (start us, length us, event | category | flops | bytes accessed | tf_op | source)
XLA Modules:
  0.0 605.0 jit_solution(1876608606432124029)
XLA Ops:
  8.4 5.2 collective-permute-start.8
  16.8 5.0 fusion.98
  25.8 4.5 collective-permute-start.1
  37.5 7.4 %all-to-all-start = ((f32[64,8,128]{2,0,1:T(8,128)}), f32[64,8,128]{2,0,1:T(8,128)}, u32[]{:S(2)}, u32[]{:S(2)}) async-start(f32[64,8,128]{2,0,1:T(8,128)} %copy.81), calls=%async_computation | async-start | bytes 524288 | tf_op jit(solution)/shard_map/all_to_all | solution.py:35
  47.3 4.0 all-to-all-done
  53.0 3.9 pad_maximum_fusion.23
  58.2 4.0 collective-permute-start.2
  62.2 54.7 %reduce-scatter.5.cloned.1.call-done = f32[32,128]{1,0:T(8,128)} async-done(((f32[512,128]{1,0:T(8,128)}), f32[32,128]{1,0:T(8,128)}) %reduce-scatter.5.cloned.1.call-update) | async-done | bytes 16400 | tf_op jit(solution)/shard_map/reduce_scatter | solution.py:36
  119.6 4.5 collective-permute-start.16
  124.2 3.7 collective-permute-start.17
  130.4 4.4 collective-permute-done.17
  138.2 24.8 %all_gather.12 = f32[512,128]{1,0:T(8,128)} all-gather(f32[32,128]{1,0:T(8,128)S(1)} %get-tuple-element.111), channel_id=1, replica_groups=mesh['tx'=8,'ty'=16] {'ty'}, dimensions={0}, use_global_device_ids=true | all-gather | bytes 278528 | tf_op jit(solution)/shard_map/all_gather | solution.py:65
  163.0 6.5 %all-to-all-start.1 = ((f32[8,64,128]{2,1,0:T(8,128)}), f32[8,64,128]{2,1,0:T(8,128)}, u32[]{:S(2)}, u32[]{:S(2)}) async-start(f32[8,64,128]{2,1,0:T(8,128)} %bitcast.211), calls=%async_computation.2 | async-start | bytes 524288 | tf_op jit(solution)/shard_map/all_to_all | solution.py:66
  172.0 5.1 pad_maximum_fusion
  185.6 7.2 %all-to-all-start.2 = ((f32[64,8,128]{2,0,1:T(8,128)}), f32[64,8,128]{2,0,1:T(8,128)}, u32[]{:S(2)}, u32[]{:S(2)}) async-start(f32[64,8,128]{2,0,1:T(8,128)} %copy.86), calls=%async_computation.3 | async-start | bytes 524288 | tf_op jit(solution)/shard_map/all_to_all | solution.py:35
  193.0 3.7 fusion.45
  197.4 5.2 collective-permute-start.5
  206.4 4.7 collective-permute-done.4
  211.1 3.9 pad_maximum_fusion.18
  216.3 3.9 collective-permute-start.6
  220.2 46.5 %reduce-scatter.7.cloned.1.call-done = f32[32,128]{1,0:T(8,128)} async-done(((f32[512,128]{1,0:T(8,128)}), f32[32,128]{1,0:T(8,128)}) %reduce-scatter.7.cloned.1.call-update) | async-done | bytes 16400 | tf_op jit(solution)/shard_map/reduce_scatter | solution.py:36
  269.4 4.6 collective-permute-start.24
  274.1 3.6 collective-permute-start.25
  280.2 4.4 collective-permute-done.25
  288.0 24.9 %all_gather.13 = f32[512,128]{1,0:T(8,128)} all-gather(f32[32,128]{1,0:T(8,128)S(1)} %get-tuple-element.109), channel_id=1, replica_groups=mesh['tx'=8,'ty'=16] {'ty'}, dimensions={0}, use_global_device_ids=true | all-gather | bytes 278528 | tf_op jit(solution)/shard_map/all_gather | solution.py:65
  312.9 5.9 all-to-all-start.3
  322.3 5.1 pad_maximum_fusion.1
  334.8 7.2 %all-to-all-start.4 = ((f32[64,8,128]{2,0,1:T(8,128)}), f32[64,8,128]{2,0,1:T(8,128)S(1)}, u32[]{:S(2)}, u32[]{:S(2)}) async-start(f32[64,8,128]{2,0,1:T(8,128)} %copy.91), calls=%async_computation.6 | async-start | bytes 524288 | tf_op jit(solution)/shard_map/all_to_all | solution.py:35
  342.0 3.7 fusion.43
  346.3 5.2 collective-permute-start.13
  354.4 5.6 collective-permute-done.12
  360.1 3.9 pad_maximum_fusion.13
  365.2 4.1 collective-permute-start.14
  369.4 45.2 %reduce-scatter.9.cloned.1.call-done = f32[32,128]{1,0:T(8,128)} async-done(((f32[512,128]{1,0:T(8,128)}), f32[32,128]{1,0:T(8,128)}) %reduce-scatter.9.cloned.1.call-update) | async-done | bytes 16400 | tf_op jit(solution)/shard_map/reduce_scatter | solution.py:36
  418.1 4.8 collective-permute-start.28
  426.4 18.5 %all_gather.14 = f32[512,128]{1,0:T(8,128)} all-gather(f32[32,128]{1,0:T(8,128)S(1)} %get-tuple-element.107), channel_id=1, replica_groups=mesh['tx'=8,'ty'=16] {'ty'}, dimensions={0}, use_global_device_ids=true | all-gather | bytes 278528 | tf_op jit(solution)/shard_map/all_gather | solution.py:65
  444.9 9.5 %all-to-all-start.5 = ((f32[8,64,128]{2,1,0:T(8,128)}), f32[8,64,128]{2,1,0:T(8,128)}, u32[]{:S(2)}, u32[]{:S(2)}) async-start(f32[8,64,128]{2,1,0:T(8,128)} %bitcast.210), calls=%async_computation.8 | async-start | bytes 524288 | tf_op jit(solution)/shard_map/all_to_all | solution.py:66
  459.1 5.1 pad_maximum_fusion.2
  472.6 7.2 %all-to-all-start.6 = ((f32[64,8,128]{2,0,1:T(8,128)}), f32[64,8,128]{2,0,1:T(8,128)}, u32[]{:S(2)}, u32[]{:S(2)}) async-start(f32[64,8,128]{2,0,1:T(8,128)} %copy.96), calls=%async_computation.9 | async-start | bytes 524288 | tf_op jit(solution)/shard_map/all_to_all | solution.py:35
  479.8 3.7 fusion.41
  484.1 5.2 collective-permute-start.21
  493.2 5.2 collective-permute-done.20
  498.4 3.9 pad_maximum_fusion.8
  503.5 3.9 collective-permute-start.22
  509.9 44.8 %reduce-scatter.11.cloned.1.call-done = f32[32,128]{1,0:T(8,128)} async-done(((f32[512,128]{1,0:T(8,128)}), f32[32,128]{1,0:T(8,128)}) %reduce-scatter.11.cloned.1.call-update) | async-done | bytes 16400 | tf_op jit(solution)/shard_map/reduce_scatter | solution.py:36
  556.0 18.6 %all_gather.15 = f32[512,128]{1,0:T(8,128)} all-gather(f32[32,128]{1,0:T(8,128)S(1)} %get-tuple-element.105), channel_id=1, replica_groups=mesh['tx'=8,'ty'=16] {'ty'}, dimensions={0}, use_global_device_ids=true | all-gather | bytes 278528 | tf_op jit(solution)/shard_map/all_gather | solution.py:65
  574.6 7.3 %all-to-all-start.7 = ((f32[8,64,128]{2,1,0:T(8,128)}), f32[8,64,128]{2,1,0:T(8,128)}, u32[]{:S(2)}, u32[]{:S(2)}) async-start(f32[8,64,128]{2,1,0:T(8,128)} %bitcast.213), calls=%async_computation.11 | async-start | bytes 524288 | tf_op jit(solution)/shard_map/all_to_all | solution.py:66
  583.8 5.1 pad_maximum_fusion.3
  (150 shorter events, 111.2 us)
Async XLA Ops:
  8.4 13.4 %copy-start.7 = (f32[4,64,1024]{2,1,0:T(8,128)S(1)}, f32[4,64,1024]{2,1,0:T(8,128)}, u32[]{:S(2)}) copy-start(f32[4,64,1024]{2,1,0:T(8,128)} %param.22) | copy-start | bytes 3145732
  8.4 24.8 %collective-permute-start.8 = (f32[16,32,1]{2,1,0:T(8,128)S(1)}, f32[16,32,1]{2,1,0:T(8,128)S(1)}, u32[]{:S(2)}, u32[]{:S(2)}) collective-permute-start(f32[16,32,1]{2,1,0:T(8,128)S(1)} %get-tuple-element.181), channel_id=1, source_target_pairs={{0,16},{16,32},{32,48},{48,64},{64,80},{80,96},{96,112},{1,17},{17... | collective-permute-start | bytes 6152 | tf_op jit(solution)/shard_map/ppermute | solution.py:21
  13.6 19.6 %collective-permute-start.9 = (f32[16,32,1]{2,1,0:T(8,128)S(1)}, f32[16,32,1]{2,1,0:T(8,128)S(1)}, u32[]{:S(2)}, u32[]{:S(2)}) collective-permute-start(f32[16,32,1]{2,1,0:T(8,128)S(1)} %get-tuple-element.180), channel_id=1, source_target_pairs={{16,0},{32,16},{48,32},{64,48},{80,64},{96,80},{112,96},{17,1},{33... | collective-permute-start | bytes 6152 | tf_op jit(solution)/shard_map/ppermute | solution.py:24
  25.1 91.7 %copy-start.14 = (s32[32,128]{1,0:T(8,128)S(1)}, s32[32,128]{1,0:T(8,128)}, u32[]{:S(2)}) copy-start(s32[32,128]{1,0:T(8,128)} %param.27) | copy-start | bytes 49156
  25.8 27.2 %collective-permute-start.1 = (f32[3,4,1,1024]{3,1,2,0:T(4,128)}, f32[3,4,1,1024]{3,1,2,0:T(4,128)S(1)}, u32[]{:S(2)}, u32[]{:S(2)}) collective-permute-start(f32[3,4,1,1024]{3,1,2,0:T(4,128)} %get-tuple-element.151), channel_id=1, source_target_pairs={{16,0},{32,16},{48,32},{64,48},{80,64},{96,80},{112,96},{17,1},{33... | collective-permute-start | bytes 147464 | tf_op jit(solution)/shard_map/ppermute | solution.py:24
  30.3 22.7 %collective-permute-start = (f32[3,4,1,1024]{3,1,2,0:T(4,128)}, f32[3,4,1,1024]{3,1,2,0:T(4,128)S(1)}, u32[]{:S(2)}, u32[]{:S(2)}) collective-permute-start(f32[3,4,1,1024]{3,1,2,0:T(4,128)} %get-tuple-element.150), channel_id=1, source_target_pairs={{0,16},{16,32},{32,48},{48,64},{64,80},{80,96},{96,112},{1,17},{17... | collective-permute-start | bytes 147464 | tf_op jit(solution)/shard_map/ppermute | solution.py:21
  34.0 10.9 %collective-permute-start.11 = (f32[16,1,130]{2,1,0:T(1,128)}, f32[16,1,130]{2,1,0:T(1,128)S(1)}, u32[]{:S(2)}, u32[]{:S(2)}) collective-permute-start(f32[16,1,130]{2,1,0:T(1,128)} %get-tuple-element.173), channel_id=1, source_target_pairs={{0,1},{1,2},{2,3},{3,4},{4,5},{5,6},{6,7},{7,8},{8,9},{9,10},{10,1... | collective-permute-start | bytes 24968 | tf_op jit(solution)/shard_map/ppermute | solution.py:21
  35.3 9.6 %collective-permute-start.10 = (f32[16,1,130]{2,1,0:T(1,128)}, f32[16,1,130]{2,1,0:T(1,128)S(1)}, u32[]{:S(2)}, u32[]{:S(2)}) collective-permute-start(f32[16,1,130]{2,1,0:T(1,128)} %get-tuple-element.172), channel_id=1, source_target_pairs={{1,0},{2,1},{3,2},{4,3},{5,4},{6,5},{7,6},{8,7},{9,8},{10,9},{11,1... | collective-permute-start | bytes 24968 | tf_op jit(solution)/shard_map/ppermute | solution.py:24
  37.5 13.8 %all-to-all-start = ((f32[64,8,128]{2,0,1:T(8,128)}), f32[64,8,128]{2,0,1:T(8,128)}, u32[]{:S(2)}, u32[]{:S(2)}) async-start(f32[64,8,128]{2,0,1:T(8,128)} %copy.81), calls=%async_computation | async-start | bytes 524288 | tf_op jit(solution)/shard_map/all_to_all | solution.py:35
  44.9 72.0 %reduce-scatter.5.cloned.1.call-start = ((), (), s32[]{:S(2)}) async-start(), calls=%async_computation.12 | async-start | bytes 278528 | tf_op jit(solution)/shard_map/reduce_scatter | solution.py:36
  56.9 115.0 %collective-permute-start.3 = (f32[3,1,66,1024]{3,1,2,0:T(1,128)}, f32[3,1,66,1024]{3,1,2,0:T(1,128)}, u32[]{:S(2)}, u32[]{:S(2)}) collective-permute-start(f32[3,1,66,1024]{3,1,2,0:T(1,128)} %get-tuple-element.143), channel_id=1, source_target_pairs={{1,0},{2,1},{3,2},{4,3},{5,4},{6,5},{7,6},{8,7},{9,8},{10,9},{11,1... | collective-permute-start | bytes 2433032 | tf_op jit(solution)/shard_map/ppermute | solution.py:24
  58.2 113.7 %collective-permute-start.2 = (f32[3,1,66,1024]{3,1,2,0:T(1,128)}, f32[3,1,66,1024]{3,1,2,0:T(1,128)}, u32[]{:S(2)}, u32[]{:S(2)}) collective-permute-start(f32[3,1,66,1024]{3,1,2,0:T(1,128)} %get-tuple-element.142), channel_id=1, source_target_pairs={{0,1},{1,2},{2,3},{3,4},{4,5},{5,6},{6,7},{7,8},{8,9},{9,10},{10,1... | collective-permute-start | bytes 2433032 | tf_op jit(solution)/shard_map/ppermute | solution.py:21
  119.6 10.8 %collective-permute-start.16 = (f32[16,32,1]{2,1,0:T(8,128)S(1)}, f32[16,32,1]{2,1,0:T(8,128)S(1)}, u32[]{:S(2)}, u32[]{:S(2)}) collective-permute-start(f32[16,32,1]{2,1,0:T(8,128)S(1)} %get-tuple-element.179), channel_id=1, source_target_pairs={{0,16},{16,32},{32,48},{48,64},{64,80},{80,96},{96,112},{1,17},{17... | collective-permute-start | bytes 6152 | tf_op jit(solution)/shard_map/ppermute | solution.py:21
  124.2 10.6 %collective-permute-start.17 = (f32[16,32,1]{2,1,0:T(8,128)S(1)}, f32[16,32,1]{2,1,0:T(8,128)S(1)}, u32[]{:S(2)}, u32[]{:S(2)}) collective-permute-start(f32[16,32,1]{2,1,0:T(8,128)S(1)} %get-tuple-element.178), channel_id=1, source_target_pairs={{16,0},{32,16},{48,32},{64,48},{80,64},{96,80},{112,96},{17,1},{33... | collective-permute-start | bytes 6152 | tf_op jit(solution)/shard_map/ppermute | solution.py:24
  135.6 33.9 %collective-permute-start.19 = (f32[16,1,130]{2,1,0:T(1,128)}, f32[16,1,130]{2,1,0:T(1,128)S(1)}, u32[]{:S(2)}, u32[]{:S(2)}) collective-permute-start(f32[16,1,130]{2,1,0:T(1,128)} %get-tuple-element.171), channel_id=1, source_target_pairs={{0,1},{1,2},{2,3},{3,4},{4,5},{5,6},{6,7},{7,8},{8,9},{9,10},{10,1... | collective-permute-start | bytes 24968 | tf_op jit(solution)/shard_map/ppermute | solution.py:21
  136.9 32.7 %collective-permute-start.18 = (f32[16,1,130]{2,1,0:T(1,128)}, f32[16,1,130]{2,1,0:T(1,128)S(1)}, u32[]{:S(2)}, u32[]{:S(2)}) collective-permute-start(f32[16,1,130]{2,1,0:T(1,128)} %get-tuple-element.170), channel_id=1, source_target_pairs={{1,0},{2,1},{3,2},{4,3},{5,4},{6,5},{7,6},{8,7},{9,8},{10,9},{11,1... | collective-permute-start | bytes 24968 | tf_op jit(solution)/shard_map/ppermute | solution.py:24
  163.0 18.4 %all-to-all-start.1 = ((f32[8,64,128]{2,1,0:T(8,128)}), f32[8,64,128]{2,1,0:T(8,128)}, u32[]{:S(2)}, u32[]{:S(2)}) async-start(f32[8,64,128]{2,1,0:T(8,128)} %bitcast.211), calls=%async_computation.2 | async-start | bytes 524288 | tf_op jit(solution)/shard_map/all_to_all | solution.py:66
  185.6 19.1 %all-to-all-start.2 = ((f32[64,8,128]{2,0,1:T(8,128)}), f32[64,8,128]{2,0,1:T(8,128)}, u32[]{:S(2)}, u32[]{:S(2)}) async-start(f32[64,8,128]{2,0,1:T(8,128)} %copy.86), calls=%async_computation.3 | async-start | bytes 524288 | tf_op jit(solution)/shard_map/all_to_all | solution.py:35
  192.9 73.9 %reduce-scatter.7.cloned.1.call-start = ((), (), s32[]{:S(2)}) async-start(), calls=%async_computation.13 | async-start | bytes 278528 | tf_op jit(solution)/shard_map/reduce_scatter | solution.py:36
  197.4 9.1 %collective-permute-start.5 = (f32[3,4,1,1024]{3,1,2,0:T(4,128)}, f32[3,4,1,1024]{3,1,2,0:T(4,128)S(1)}, u32[]{:S(2)}, u32[]{:S(2)}) collective-permute-start(f32[3,4,1,1024]{3,1,2,0:T(4,128)} %get-tuple-element.149), channel_id=1, source_target_pairs={{16,0},{32,16},{48,32},{64,48},{80,64},{96,80},{112,96},{17,1},{33... | collective-permute-start | bytes 147464 | tf_op jit(solution)/shard_map/ppermute | solution.py:24
  202.5 8.6 %collective-permute-start.4 = (f32[3,4,1,1024]{3,1,2,0:T(4,128)}, f32[3,4,1,1024]{3,1,2,0:T(4,128)S(1)}, u32[]{:S(2)}, u32[]{:S(2)}) collective-permute-start(f32[3,4,1,1024]{3,1,2,0:T(4,128)} %get-tuple-element.148), channel_id=1, source_target_pairs={{0,16},{16,32},{32,48},{48,64},{64,80},{80,96},{96,112},{1,17},{17... | collective-permute-start | bytes 147464 | tf_op jit(solution)/shard_map/ppermute | solution.py:21
  215.0 107.2 %collective-permute-start.7 = (f32[3,1,66,1024]{3,1,2,0:T(1,128)}, f32[3,1,66,1024]{3,1,2,0:T(1,128)}, u32[]{:S(2)}, u32[]{:S(2)}) collective-permute-start(f32[3,1,66,1024]{3,1,2,0:T(1,128)} %get-tuple-element.141), channel_id=1, source_target_pairs={{1,0},{2,1},{3,2},{4,3},{5,4},{6,5},{7,6},{8,7},{9,8},{10,9},{11,1... | collective-permute-start | bytes 2433032 | tf_op jit(solution)/shard_map/ppermute | solution.py:24
  216.3 106.0 %collective-permute-start.6 = (f32[3,1,66,1024]{3,1,2,0:T(1,128)}, f32[3,1,66,1024]{3,1,2,0:T(1,128)}, u32[]{:S(2)}, u32[]{:S(2)}) collective-permute-start(f32[3,1,66,1024]{3,1,2,0:T(1,128)} %get-tuple-element.140), channel_id=1, source_target_pairs={{0,1},{1,2},{2,3},{3,4},{4,5},{5,6},{6,7},{7,8},{8,9},{9,10},{10,1... | collective-permute-start | bytes 2433032 | tf_op jit(solution)/shard_map/ppermute | solution.py:21
  269.3 15.3 %copy-start = (f32[16,32,128]{2,1,0:T(8,128)}, f32[16,32,128]{2,1,0:T(8,128)S(1)}, u32[]{:S(2)}) copy-start(f32[16,32,128]{2,1,0:T(8,128)S(1)} %fusion.78) | copy-start | bytes 786436
  269.4 10.8 %collective-permute-start.24 = (f32[16,32,1]{2,1,0:T(8,128)S(1)}, f32[16,32,1]{2,1,0:T(8,128)S(1)}, u32[]{:S(2)}, u32[]{:S(2)}) collective-permute-start(f32[16,32,1]{2,1,0:T(8,128)S(1)} %get-tuple-element.177), channel_id=1, source_target_pairs={{0,16},{16,32},{32,48},{48,64},{64,80},{80,96},{96,112},{1,17},{17... | collective-permute-start | bytes 6152 | tf_op jit(solution)/shard_map/ppermute | solution.py:21
  274.1 10.6 %collective-permute-start.25 = (f32[16,32,1]{2,1,0:T(8,128)S(1)}, f32[16,32,1]{2,1,0:T(8,128)S(1)}, u32[]{:S(2)}, u32[]{:S(2)}) collective-permute-start(f32[16,32,1]{2,1,0:T(8,128)S(1)} %get-tuple-element.176), channel_id=1, source_target_pairs={{16,0},{32,16},{48,32},{64,48},{80,64},{96,80},{112,96},{17,1},{33... | collective-permute-start | bytes 6152 | tf_op jit(solution)/shard_map/ppermute | solution.py:24
  280.2 32.7 %copy-start.11 = (f32[16,32,1]{2,1,0:T(8,128)}, f32[16,32,1]{2,1,0:T(8,128)S(1)}, u32[]{:S(2)}) copy-start(f32[16,32,1]{2,1,0:T(8,128)S(1)} %collective-permute-done.24) | copy-start | bytes 6148
  285.4 33.5 %collective-permute-start.27 = (f32[16,1,130]{2,1,0:T(1,128)}, f32[16,1,130]{2,1,0:T(1,128)S(1)}, u32[]{:S(2)}, u32[]{:S(2)}) collective-permute-start(f32[16,1,130]{2,1,0:T(1,128)} %get-tuple-element.169), channel_id=1, source_target_pairs={{0,1},{1,2},{2,3},{3,4},{4,5},{5,6},{6,7},{7,8},{8,9},{9,10},{10,1... | collective-permute-start | bytes 24968 | tf_op jit(solution)/shard_map/ppermute | solution.py:21
  286.7 32.2 %collective-permute-start.26 = (f32[16,1,130]{2,1,0:T(1,128)}, f32[16,1,130]{2,1,0:T(1,128)S(1)}, u32[]{:S(2)}, u32[]{:S(2)}) collective-permute-start(f32[16,1,130]{2,1,0:T(1,128)} %get-tuple-element.168), channel_id=1, source_target_pairs={{1,0},{2,1},{3,2},{4,3},{5,4},{6,5},{7,6},{8,7},{9,8},{10,9},{11,1... | collective-permute-start | bytes 24968 | tf_op jit(solution)/shard_map/ppermute | solution.py:24
  312.9 18.5 %all-to-all-start.3 = ((f32[8,64,128]{2,1,0:T(8,128)}), f32[8,64,128]{2,1,0:T(8,128)S(1)}, u32[]{:S(2)}, u32[]{:S(2)}) async-start(f32[8,64,128]{2,1,0:T(8,128)} %bitcast.212), calls=%async_computation.5 | async-start | bytes 524288 | tf_op jit(solution)/shard_map/all_to_all | solution.py:66
  334.8 18.9 %all-to-all-start.4 = ((f32[64,8,128]{2,0,1:T(8,128)}), f32[64,8,128]{2,0,1:T(8,128)S(1)}, u32[]{:S(2)}, u32[]{:S(2)}) async-start(f32[64,8,128]{2,0,1:T(8,128)} %copy.91), calls=%async_computation.6 | async-start | bytes 524288 | tf_op jit(solution)/shard_map/all_to_all | solution.py:35
  342.0 72.6 %reduce-scatter.9.cloned.1.call-start = ((), (), s32[]{:S(2)}) async-start(), calls=%async_computation.14 | async-start | bytes 278528 | tf_op jit(solution)/shard_map/reduce_scatter | solution.py:36
  346.3 8.1 %collective-permute-start.13 = (f32[3,4,1,1024]{3,1,2,0:T(4,128)}, f32[3,4,1,1024]{3,1,2,0:T(4,128)S(1)}, u32[]{:S(2)}, u32[]{:S(2)}) collective-permute-start(f32[3,4,1,1024]{3,1,2,0:T(4,128)} %get-tuple-element.147), channel_id=1, source_target_pairs={{16,0},{32,16},{48,32},{64,48},{80,64},{96,80},{112,96},{17,1},{33... | collective-permute-start | bytes 147464 | tf_op jit(solution)/shard_map/ppermute | solution.py:24
  351.5 8.6 %collective-permute-start.12 = (f32[3,4,1,1024]{3,1,2,0:T(4,128)}, f32[3,4,1,1024]{3,1,2,0:T(4,128)S(1)}, u32[]{:S(2)}, u32[]{:S(2)}) collective-permute-start(f32[3,4,1,1024]{3,1,2,0:T(4,128)} %get-tuple-element.146), channel_id=1, source_target_pairs={{0,16},{16,32},{32,48},{48,64},{64,80},{80,96},{96,112},{1,17},{17... | collective-permute-start | bytes 147464 | tf_op jit(solution)/shard_map/ppermute | solution.py:21
  364.0 95.1 %collective-permute-start.15 = (f32[3,1,66,1024]{3,1,2,0:T(1,128)}, f32[3,1,66,1024]{3,1,2,0:T(1,128)}, u32[]{:S(2)}, u32[]{:S(2)}) collective-permute-start(f32[3,1,66,1024]{3,1,2,0:T(1,128)} %get-tuple-element.139), channel_id=1, source_target_pairs={{1,0},{2,1},{3,2},{4,3},{5,4},{6,5},{7,6},{8,7},{9,8},{10,9},{11,1... | collective-permute-start | bytes 2433032 | tf_op jit(solution)/shard_map/ppermute | solution.py:24
  365.2 93.9 %collective-permute-start.14 = (f32[3,1,66,1024]{3,1,2,0:T(1,128)}, f32[3,1,66,1024]{3,1,2,0:T(1,128)}, u32[]{:S(2)}, u32[]{:S(2)}) collective-permute-start(f32[3,1,66,1024]{3,1,2,0:T(1,128)} %get-tuple-element.138), channel_id=1, source_target_pairs={{0,1},{1,2},{2,3},{3,4},{4,5},{5,6},{6,7},{7,8},{8,9},{9,10},{10,1... | collective-permute-start | bytes 2433032 | tf_op jit(solution)/shard_map/ppermute | solution.py:21
  418.1 36.3 %collective-permute-start.28 = (f32[16,32,1]{2,1,0:T(8,128)}, f32[16,32,1]{2,1,0:T(8,128)}, u32[]{:S(2)}, u32[]{:S(2)}) collective-permute-start(f32[16,32,1]{2,1,0:T(8,128)} %get-tuple-element.175), channel_id=1, source_target_pairs={{0,16},{16,32},{32,48},{48,64},{64,80},{80,96},{96,112},{1,17},{17... | collective-permute-start | bytes 6152 | tf_op jit(solution)/shard_map/ppermute | solution.py:21
  422.9 31.5 %collective-permute-start.29 = (f32[16,32,1]{2,1,0:T(8,128)}, f32[16,32,1]{2,1,0:T(8,128)}, u32[]{:S(2)}, u32[]{:S(2)}) collective-permute-start(f32[16,32,1]{2,1,0:T(8,128)} %get-tuple-element.174), channel_id=1, source_target_pairs={{16,0},{32,16},{48,32},{64,48},{80,64},{96,80},{112,96},{17,1},{33... | collective-permute-start | bytes 6152 | tf_op jit(solution)/shard_map/ppermute | solution.py:24
  444.9 23.3 %all-to-all-start.5 = ((f32[8,64,128]{2,1,0:T(8,128)}), f32[8,64,128]{2,1,0:T(8,128)}, u32[]{:S(2)}, u32[]{:S(2)}) async-start(f32[8,64,128]{2,1,0:T(8,128)} %bitcast.210), calls=%async_computation.8 | async-start | bytes 524288 | tf_op jit(solution)/shard_map/all_to_all | solution.py:66
  456.1 51.4 %collective-permute-start.31 = (f32[16,1,130]{2,1,0:T(1,128)}, f32[16,1,130]{2,1,0:T(1,128)S(1)}, u32[]{:S(2)}, u32[]{:S(2)}) collective-permute-start(f32[16,1,130]{2,1,0:T(1,128)} %get-tuple-element.167), channel_id=1, source_target_pairs={{0,1},{1,2},{2,3},{3,4},{4,5},{5,6},{6,7},{7,8},{8,9},{9,10},{10,1... | collective-permute-start | bytes 24968 | tf_op jit(solution)/shard_map/ppermute | solution.py:21
  457.8 49.7 %collective-permute-start.30 = (f32[16,1,130]{2,1,0:T(1,128)}, f32[16,1,130]{2,1,0:T(1,128)S(1)}, u32[]{:S(2)}, u32[]{:S(2)}) collective-permute-start(f32[16,1,130]{2,1,0:T(1,128)} %get-tuple-element.166), channel_id=1, source_target_pairs={{1,0},{2,1},{3,2},{4,3},{5,4},{6,5},{7,6},{8,7},{9,8},{10,9},{11,1... | collective-permute-start | bytes 24968 | tf_op jit(solution)/shard_map/ppermute | solution.py:24
  472.6 18.9 %all-to-all-start.6 = ((f32[64,8,128]{2,0,1:T(8,128)}), f32[64,8,128]{2,0,1:T(8,128)}, u32[]{:S(2)}, u32[]{:S(2)}) async-start(f32[64,8,128]{2,0,1:T(8,128)} %copy.96), calls=%async_computation.9 | async-start | bytes 524288 | tf_op jit(solution)/shard_map/all_to_all | solution.py:35
  479.8 74.9 %reduce-scatter.11.cloned.1.call-start = ((), (), s32[]{:S(2)}) async-start(), calls=%async_computation.15 | async-start | bytes 278528 | tf_op jit(solution)/shard_map/reduce_scatter | solution.py:36
  484.1 9.1 %collective-permute-start.21 = (f32[3,4,1,1024]{3,1,2,0:T(4,128)}, f32[3,4,1,1024]{3,1,2,0:T(4,128)S(1)}, u32[]{:S(2)}, u32[]{:S(2)}) collective-permute-start(f32[3,4,1,1024]{3,1,2,0:T(4,128)} %get-tuple-element.145), channel_id=1, source_target_pairs={{16,0},{32,16},{48,32},{64,48},{80,64},{96,80},{112,96},{17,1},{33... | collective-permute-start | bytes 147464 | tf_op jit(solution)/shard_map/ppermute | solution.py:24
  489.3 9.1 %collective-permute-start.20 = (f32[3,4,1,1024]{3,1,2,0:T(4,128)}, f32[3,4,1,1024]{3,1,2,0:T(4,128)S(1)}, u32[]{:S(2)}, u32[]{:S(2)}) collective-permute-start(f32[3,4,1,1024]{3,1,2,0:T(4,128)} %get-tuple-element.144), channel_id=1, source_target_pairs={{0,16},{16,32},{32,48},{48,64},{64,80},{80,96},{96,112},{1,17},{17... | collective-permute-start | bytes 147464 | tf_op jit(solution)/shard_map/ppermute | solution.py:21
  502.2 81.6 %collective-permute-start.23 = (f32[3,1,66,1024]{3,1,2,0:T(1,128)}, f32[3,1,66,1024]{3,1,2,0:T(1,128)}, u32[]{:S(2)}, u32[]{:S(2)}) collective-permute-start(f32[3,1,66,1024]{3,1,2,0:T(1,128)} %get-tuple-element.137), channel_id=1, source_target_pairs={{1,0},{2,1},{3,2},{4,3},{5,4},{6,5},{7,6},{8,7},{9,8},{10,9},{11,1... | collective-permute-start | bytes 2433032 | tf_op jit(solution)/shard_map/ppermute | solution.py:24
  503.5 80.3 %collective-permute-start.22 = (f32[3,1,66,1024]{3,1,2,0:T(1,128)}, f32[3,1,66,1024]{3,1,2,0:T(1,128)}, u32[]{:S(2)}, u32[]{:S(2)}) collective-permute-start(f32[3,1,66,1024]{3,1,2,0:T(1,128)} %get-tuple-element.136), channel_id=1, source_target_pairs={{0,1},{1,2},{2,3},{3,4},{4,5},{5,6},{6,7},{7,8},{8,9},{9,10},{10,1... | collective-permute-start | bytes 2433032 | tf_op jit(solution)/shard_map/ppermute | solution.py:21
  574.6 18.4 %all-to-all-start.7 = ((f32[8,64,128]{2,1,0:T(8,128)}), f32[8,64,128]{2,1,0:T(8,128)}, u32[]{:S(2)}, u32[]{:S(2)}) async-start(f32[8,64,128]{2,1,0:T(8,128)} %bitcast.213), calls=%async_computation.11 | async-start | bytes 524288 | tf_op jit(solution)/shard_map/all_to_all | solution.py:66
  (11 other events, 30.7 us)
Sparse Core Ops, SparseCore 0:
  53.1 63.6 reduce-scatter.4
  206.6 60.1 reduce-scatter.6
  354.6 59.9 reduce-scatter.8
  493.3 61.3 reduce-scatter.10
where the time goes:
time: 616 us; the launch traced here: 605 us
  waiting for transfers between devices  225 us (37%)
  starting transfers between devices  153 us (25%)
  other arithmetic  99.7 us (16%)
  blocking collectives  86.9 us (14%)
  local copies, waits for them, and re-layouts  26.2 us (4%)
  between operations  14.9 us (2%)
    reduce_scatter x4, waiting for transfers between devices, to_plate(): lax.psum_scatter(jnp.where(is_owner, spread, 0.0), 'ty', scatter_dimensio...  191 us
    all_gather x4, blocking collectives, on_device(): returned = lax.all_gather(coupling, 'ty', axis=0, tiled=True)  86.9 us
    ppermute x16, starting transfers between devices, with_halo(): lax.ppermute(lax.slice_in_dim(block, block.shape[dim] - width, None, axis...  50 us
    ppermute x16, starting transfers between devices, with_halo(): lax.ppermute(lax.slice_in_dim(block, 0, width, axis=dim), axis, backward)  44.2 us
    all_to_all x4, starting transfers between devices, on_device(): lax.all_to_all(returned, 'tx', split_axis=0, concat_axis=1, tiled=True)  29.2 us
    all_to_all x4, starting transfers between devices, to_plate(): lax.all_to_all(wall_layer, 'tx', split_axis=1, concat_axis=0, tiled=True)  29 us
    ppermute x16, waiting for transfers between devices, with_halo(): lax.ppermute(lax.slice_in_dim(block, block.shape[dim] - width, None, axis...  20.6 us
    concatenate x4, other arithmetic, with_halo(): block = jnp.concatenate([low, block, high], axis=dim)  20.3 us
  transfers between devices with their start and end apart: 44, of which 12 were waited for; matrix products, arithmetic and copies ran while one was open for 18% of the time, Pallas kernels for 0%

commit v1 on v0

v1 whole, which is shorter than its diff:
```python
import jax
import jax.numpy as jnp
from jax import lax
from jax.experimental import pallas as pl
from jax.experimental.pallas import tpu as pltpu
from jax.sharding import PartitionSpec as P

MESH = pl.DeviceIdType.MESH
STEPS = 4
PZ = 16
LAYERS = 4
ROWS = 64
BLOCKS = 8
CHUNKS = 4
PROWS = 32
LANES = 128
TX = 8
TY = 16


def kernel(
    seed_fluid, seed_plate, velocity, enthalpy, phase, contact,
    out_fluid, out_plate,
    F, V, ZS, ZR, YS, YR, CR, CC, CF, CI, PR, PT, EN, PH, PYS, PYR, PXS, PXR, SXM,
    load_f, load_v, load_p, load_e, out_sem,
    zs_sem, zr_sem, ys_sem, yr_sem, cs_sem, cr_sem, ccs_sem, ccr_sem, fs_sem, pr_sem,
    pys_sem, pyr_sem, pxs_sem, pxr_sem,
):
    tx = lax.axis_index("tx")
    ty = lax.axis_index("ty")
    has_down, has_up = ty > 0, ty < TY - 1
    has_lo, has_hi = tx > 0, tx < TX - 1
    is_wall = ty == 0
    home_tx = ty // 2
    is_self = (tx == 0) & (ty == 0)
    not_self = jnp.logical_not(is_self)
    lane = lax.broadcasted_iota(jnp.int32, (ROWS, LANES), 1)
    row = lax.broadcasted_iota(jnp.int32, (ROWS, LANES), 0)

    def lanes(b):
        return pl.ds(pl.multiple_of(b * LANES, LANES), LANES)

    f_loads = [
        pltpu.make_async_copy(seed_fluid.at[:, :, pl.ds(b * LANES, LANES)], F.at[0, b], load_f.at[b])
        for b in range(BLOCKS)
    ]
    for copy in f_loads:
        copy.start()
    for c in (2, 1, 0):
        pltpu.make_async_copy(velocity.at[STEPS - 1, c], V.at[STEPS - 1, c], load_v.at[STEPS - 1, c]).start()
    contact_load = pltpu.make_async_copy(contact, CI, load_p.at[1])
    contact_load.start()
    plate_load = pltpu.make_async_copy(seed_plate, PT.at[0], load_p.at[0])
    plate_load.start()

    def late_loads(n):
        e = pltpu.make_async_copy(enthalpy.at[n], EN.at[n], load_e.at[n, 0])
        p = pltpu.make_async_copy(phase.at[n], PH.at[n], load_e.at[n, 1])
        v = [pltpu.make_async_copy(velocity.at[n, c], V.at[n, c], load_v.at[n, c]) for c in range(3)]
        return e, p, v

    barrier = pltpu.get_barrier_semaphore()

    def greet(cond, device):
        @pl.when(cond)
        def _():
            pl.semaphore_signal(barrier, inc=1, device_id=device, device_id_type=MESH)

        return jnp.where(cond, 1, 0)

    expected = greet(not_self, (home_tx, 0))
    for c in range(TX):
        for r in range(2):
            expected += greet(is_wall & ((tx > 0) | (2 * c + r > 0)), (c, 2 * tx + r))
    expected += greet(has_lo, (tx - 1, ty))
    expected += greet(has_hi, (tx + 1, ty))
    expected += greet(has_down, (tx, ty - 1))
    expected += greet(has_up, (tx, ty + 1))

    for n in (3, 2, 1, 0):
        e, p, v = late_loads(n)
        e.start()
        p.start()
        if n < STEPS - 1:
            for copy in v:
                copy.start()

    def remote(src, dst, send, recv, device):
        return pltpu.make_async_remote_copy(
            src_ref=src, dst_ref=dst, send_sem=send, recv_sem=recv, device_id=device, device_id_type=MESH
        )

    def z_down(s, j):
        blocks = pl.ds(2 * j, 2)
        return remote(ZS.at[s, 0, blocks], ZR.at[s, 1, blocks], zs_sem.at[s, 0, j], zr_sem.at[s, 1, j], (tx, ty - 1))

    def z_up(s, j):
        blocks = pl.ds(2 * j, 2)
        return remote(ZS.at[s, 1, blocks], ZR.at[s, 0, blocks], zs_sem.at[s, 1, j], zr_sem.at[s, 0, j], (tx, ty + 1))

    def y_lo(s, j):
        return remote(YS.at[s, 0, j], YR.at[s, 1, j], ys_sem.at[s, 0, j], yr_sem.at[s, 1, j], (tx - 1, ty))

    def y_hi(s, j):
        return remote(YS.at[s, 1, j], YR.at[s, 0, j], ys_sem.at[s, 1, j], yr_sem.at[s, 0, j], (tx + 1, ty))

    def wall_out(s, j, bb, r):
        b = 2 * j + bb
        return remote(
            F.at[s, b, 0, pl.ds(PROWS * r, PROWS)], PR.at[s], fs_sem.at[s, b, r], pr_sem.at[s], (b, 2 * tx + r)
        )

    def each_wall_out(s, j, act):
        for bb in range(2):
            for r in range(2):
                away = is_wall if (bb, r) != (0, 0) else is_wall & ((tx > 0) | (j > 0))

                @pl.when(away)
                def _(bb=bb, r=r):
                    act(wall_out(s, j, bb, r))

    def launch(s, j):
        pl.when(has_lo)(lambda: y_lo(s, j).start())
        pl.when(has_hi)(lambda: y_hi(s, j).start())
        pl.when(has_down)(lambda: z_down(s, j).start())
        pl.when(has_up)(lambda: z_up(s, j).start())
        each_wall_out(s, j, lambda copy: copy.start())

        @pl.when(is_self & (j == 0))
        def _():
            pltpu.make_async_copy(F.at[s, 0, 0, pl.ds(0, PROWS)], PR.at[s], pr_sem.at[s]).start()

    def sent(s, j):
        pl.when(has_lo)(lambda: y_lo(s, j).wait_send())
        pl.when(has_hi)(lambda: y_hi(s, j).wait_send())
        pl.when(has_down)(lambda: z_down(s, j).wait_send())
        pl.when(has_up)(lambda: z_up(s, j).wait_send())
        each_wall_out(s, j, lambda copy: copy.wait_send())

    def stage(s, j):
        n = STEPS - 1 - s
        for bb in range(2):
            b = 2 * j + bb
            g = 0.1 * F[s, b, 0]
            ZS[s, 0, b] = g + g * V[n, 2, 0, :, lanes(b)].astype(jnp.float32)
            g = 0.1 * F[s, b, LAYERS - 1]
            ZS[s, 1, b] = g - g * V[n, 2, LAYERS - 1, :, lanes(b)].astype(jnp.float32)
            for l in range(LAYERS):
                q = LAYERS * bb + l
                g = 0.1 * F[s, b, l, 0:1, :]
                v = V[n, 1, l, 0:16, lanes(b)].astype(jnp.float32)[0:1]
                YS[s, 0, j, q : q + 1, :] = g + g * v
                g = 0.1 * F[s, b, l, ROWS - 1 : ROWS, :]
                v = V[n, 1, l, ROWS - 16 : ROWS, lanes(b)].astype(jnp.float32)[15:16]
                YS[s, 1, j, q : q + 1, :] = g - g * v

    def interior(s, b):
        n = STEPS - 1 - s
        before = jnp.maximum(b - 1, 0)
        pending = below = None
        for l in range(LAYERS):
            f = F[s, b, l]
            g = 0.1 * f
            gu = g * V[n, 0, l, :, lanes(b)].astype(jnp.float32)
            gv = g * V[n, 1, l, :, lanes(b)].astype(jnp.float32)
            gw = g * V[n, 2, l, :, lanes(b)].astype(jnp.float32)
            from_right = pltpu.roll(g + gu, LANES - 1, 1)
            from_left = pltpu.roll(g - gu, 1, 1)
            from_above = pltpu.roll(g + gv, ROWS - 1, 0)
            from_below = pltpu.roll(g - gv, 1, 0)
            total = 0.4 * f
            total += jnp.where(lane == LANES - 1, 0.0, from_right)
            total += jnp.where(lane == 0, jnp.where(b > 0, SXM[l], 0.0), from_left)
            total += jnp.where(row == ROWS - 1, 0.0, from_above)
            total += jnp.where(row == 0, 0.0, from_below)
            SXM[l] = from_left
            if l > 0:
                F[s + 1, b, l - 1] = pending + (g + gw)
                total += below
            below = g - gw
            pending = total
            edge = jnp.where((lane == LANES - 1) & (b > 0), from_right, 0.0)
            if l > 0:
                F[s + 1, before, l - 1] += edge_before
            edge_before = edge
        F[s + 1, b, LAYERS - 1] = pending
        F[s + 1, before, LAYERS - 1] += edge_before

    def finish(s, j):
        @pl.when(has_lo)
        def _():
            y_hi(s, j).wait_recv()
            for q in range(2 * LAYERS):
                b, l = 2 * j + q // LAYERS, q % LAYERS
                F[s + 1, b, l, 0:1, :] += YR[s, 0, j, q : q + 1, :]

        @pl.when(has_hi)
        def _():
            y_lo(s, j).wait_recv()
            for q in range(2 * LAYERS):
                b, l = 2 * j + q // LAYERS, q % LAYERS
                F[s + 1, b, l, ROWS - 1 : ROWS, :] += YR[s, 1, j, q : q + 1, :]

        @pl.when(has_down)
        def _():
            z_up(s, j).wait_recv()
            for bb in range(2):
                F[s + 1, 2 * j + bb, 0] += ZR[s, 0, 2 * j + bb]

        @pl.when(has_up)
        def _():
            z_down(s, j).wait_recv()
            for bb in range(2):
                F[s + 1, 2 * j + bb, LAYERS - 1] += ZR[s, 1, 2 * j + bb]

        @pl.when(is_wall)
        def _():
            blocks = pl.ds(2 * j, 2)
            pltpu.make_async_copy(CR.at[s, blocks], CR.at[s, blocks], cr_sem.at[s, j]).wait()

            @pl.when(s == 0)
            def _():
                pltpu.make_async_copy(CC.at[blocks], CC.at[blocks], ccr_sem.at[j]).wait()

            for bb in range(2):
                b = 2 * j + bb
                F[s + 1, b, 0] += CC[b] * (0.5 * CR[s, b] - 0.5 * F[s, b, 0])

    tile_rows = pl.ds(pl.multiple_of(PROWS * lax.rem(ty, 2), PROWS), PROWS)
    tile_chunk = tx // 2

    def wall_in(s):
        return remote(
            PT.at[s, PZ - 1], CR.at[s, tx, tile_rows], cs_sem.at[s], cr_sem.at[s, tile_chunk], (home_tx, 0)
        )

    def contact_in():
        return remote(CF, CC.at[tx, tile_rows], ccs_sem.at[0], ccr_sem.at[tile_chunk], (home_tx, 0))

    def py_lo(s):
        return remote(PYS.at[s, 0], PYR.at[s, 1], pys_sem.at[s, 0], pyr_sem.at[s, 1], (tx, ty - 1))

    def py_hi(s):
        return remote(PYS.at[s, 1], PYR.at[s, 0], pys_sem.at[s, 1], pyr_sem.at[s, 0], (tx, ty + 1))

    def px_lo(s):
        return remote(PXS.at[s], PXR.at[s, 1], pxs_sem.at[s, 0], pxr_sem.at[s, 1], (tx - 1, ty))

    def px_hi(s):
        return remote(PXS.at[s], PXR.at[s, 0], pxs_sem.at[s, 1], pxr_sem.at[s, 0], (tx + 1, ty))

    def plate_launch(s):
        pl.when(not_self)(lambda: wall_in(s).start())

        @pl.when(is_self)
        def _():
            pltpu.make_async_copy(PT.at[s, PZ - 1], CR.at[s, 0, pl.ds(0, PROWS)], cr_sem.at[s, 0]).start()

        pl.when(has_lo)(lambda: px_lo(s).start())
        pl.when(has_hi)(lambda: px_hi(s).start())
        pl.when(has_down)(lambda: py_lo(s).start())
        pl.when(has_up)(lambda: py_hi(s).start())

    def plate_sent(s):
        pl.when(not_self)(lambda: wall_in(s).wait_send())
        pl.when(has_lo)(lambda: px_lo(s).wait_send())
        pl.when(has_hi)(lambda: px_hi(s).wait_send())
        pl.when(has_down)(lambda: py_lo(s).wait_send())
        pl.when(has_up)(lambda: py_hi(s).wait_send())

    small_lane = lax.broadcasted_iota(jnp.int32, (8, LANES), 1)

    def edge_rows(s, z, value):
        PYS[s, 0, pl.ds(z, 1), :] = value[0:1]
        PYS[s, 1, pl.ds(z, 1), :] = value[PROWS - 1 : PROWS]

    def edge_columns(packed, z, value):
        for k in range(PROWS // 8):
            part = value[8 * k : 8 * k + 8]
            place = 16 * k + z
            packed = jnp.where(small_lane == place, pltpu.roll(part, place, 1), packed)
            packed = jnp.where(small_lane == place + 64, pltpu.roll(part, place + 65, 1), packed)
        return packed

    def plate_stage(s):
        def body(z, packed):
            value = PT[s, z]
            edge_rows(s, z, value)
            return edge_columns(packed, z, value)

        PXS[s] = lax.fori_loop(0, PZ, body, jnp.zeros((8, LANES), jnp.float32))

    plate_lane = lax.broadcasted_iota(jnp.int32, (PROWS, LANES), 1)
    plate_row = lax.broadcasted_iota(jnp.int32, (PROWS, LANES), 0)

    def plate_step(s):
        n = STEPS - 1 - s
        pltpu.make_async_copy(PR.at[s], PR.at[s], pr_sem.at[s]).wait()
        pl.when(has_lo)(lambda: px_hi(s).wait_recv())
        pl.when(has_hi)(lambda: px_lo(s).wait_recv())
        pl.when(has_down)(lambda: py_hi(s).wait_recv())
        pl.when(has_up)(lambda: py_lo(s).wait_recv())
        e, p, _ = late_loads(n)
        e.wait()
        p.wait()
        from_lo, from_hi = PXR[s, 0], PXR[s, 1]
        coupling = CF[...] * (0.5 * PT[s, PZ - 1] - 0.5 * PR[s])

        def body(z, packed):
            value = PT[s, z]
            left = [pltpu.roll(from_lo, 64 - 16 * k - z, 1) for k in range(PROWS // 8)]
            right = [pltpu.roll(from_hi, LANES - 1 - 16 * k - z, 1) for k in range(PROWS // 8)]
            total = jnp.where(plate_lane == 0, jnp.concatenate(left, 0), pltpu.roll(value, 1, 1))
            total += jnp.where(
                plate_lane == LANES - 1, jnp.concatenate(right, 0), pltpu.roll(value, LANES - 1, 1)
            )
            total += jnp.where(plate_row == 0, PYR[s, 0, pl.ds(z, 1), :], pltpu.roll(value, 1, 0))
            total += jnp.where(
                plate_row == PROWS - 1, PYR[s, 1, pl.ds(z, 1), :], pltpu.roll(value, PROWS - 1, 0)
            )
            total += jnp.where(z > 0, PT[s, jnp.maximum(z - 1, 0)], 0.0)
            total += jnp.where(z < PZ - 1, PT[s, jnp.minimum(z + 1, PZ - 1)], 0.0)
            forcing = 0.12 * (total - 6.0 * value) - jnp.where(z == PZ - 1, coupling, 0.0)
            saved = EN[n, z]
            state = PH[n, z]
            slopes = 1.0 / (1.0 + 8.0 * saved * (1.0 - saved))
            slopes = jnp.where(state == 0, 1.0, jnp.where(state == 2, 0.7, slopes))
            value = value + slopes * forcing
            PT[s + 1, z] = value
            edge_rows(s + 1, z, value)
            return edge_columns(packed, z, value)

        packed = lax.fori_loop(0, PZ, body, jnp.zeros((8, LANES), jnp.float32))

        @pl.when(s < STEPS - 1)
        def _():
            PXS[s + 1] = packed
            plate_launch(s + 1)

        plate_sent(s)

        @pl.when(s == STEPS - 1)
        def _():
            pltpu.make_async_copy(PT.at[STEPS], out_plate, out_sem.at[CHUNKS]).start()

    for absent, side in ((ty == 0, 0), (ty == TY - 1, 1)):
        @pl.when(absent)
        def _(side=side):
            for s in range(STEPS):
                PYR[s, side] = jnp.zeros((PZ, LANES), jnp.float32)

    for absent, side in ((tx == 0, 0), (tx == TX - 1, 1)):
        @pl.when(absent)
        def _(side=side):
            for s in range(STEPS):
                PXR[s, side] = jnp.zeros((8, LANES), jnp.float32)

    contact_load.wait()
    CF[...] = CI[...].astype(jnp.float32)
    for copy in f_loads:
        copy.wait()
    for c in (2, 1, 0):
        pltpu.make_async_copy(velocity.at[STEPS - 1, c], V.at[STEPS - 1, c], load_v.at[STEPS - 1, c]).wait()

    def first_stage(j, carry):
        stage(0, j)
        return carry

    lax.fori_loop(0, CHUNKS, first_stage, 0)
    plate_load.wait()
    plate_stage(0)
    pl.semaphore_wait(barrier, expected)

    pl.when(not_self)(lambda: contact_in().start())

    @pl.when(is_self)
    def _():
        pltpu.make_async_copy(CF, CC.at[0, pl.ds(0, PROWS)], ccr_sem.at[0]).start()

    plate_launch(0)

    def first_launch(j, carry):
        launch(0, j)
        return carry

    lax.fori_loop(0, CHUNKS, first_launch, 0)

    def first_interior(b, carry):
        interior(0, b)
        return carry

    lax.fori_loop(0, BLOCKS, first_interior, 0)

    def slot(t, carry):
        s, j = t // CHUNKS, lax.rem(t, CHUNKS)
        finish(s, j)

        @pl.when(s < STEPS - 1)
        def _():
            @pl.when(j == 0)
            def _():
                for copy in late_loads(STEPS - 2 - s)[2]:
                    copy.wait()

            stage(s + 1, j)
            launch(s + 1, j)

            def body(bb, c):
                interior(s + 1, 2 * j + bb)
                return c

            lax.fori_loop(0, 2, body, 0)

        @pl.when(s == STEPS - 1)
        def _():
            where = pl.ds(pl.multiple_of(2 * LANES * j, 2 * LANES), 2 * LANES)
            for bb in range(2):
                b = 2 * j + bb
                pltpu.make_async_copy(F.at[STEPS, b], out_fluid.at[:, :, lanes(b)], out_sem.at[j]).start()

        sent(s, j)
        for step in range(STEPS):
            @pl.when(t == jnp.maximum(CHUNKS * step + tile_chunk - 1, 1))
            def _(step=step):
                plate_step(step)

        return carry

    lax.fori_loop(0, STEPS * CHUNKS, slot, 0)

    pl.when(not_self)(lambda: contact_in().wait_send())
    for j in range(CHUNKS):
        pltpu.make_async_copy(F.at[STEPS, pl.ds(2 * j, 2)], F.at[STEPS, pl.ds(2 * j, 2)], out_sem.at[j]).wait()
    pltpu.make_async_copy(PT.at[STEPS], out_plate, out_sem.at[CHUNKS]).wait()


def on_device(seed_fluid, seed_plate, velocity, enthalpy, phase, contact):
    f32 = jnp.float32
    dma = pltpu.SemaphoreType.DMA
    return pl.pallas_call(
        kernel,
        out_shape=(
            jax.ShapeDtypeStruct(seed_fluid.shape, f32),
            jax.ShapeDtypeStruct(seed_plate.shape, f32),
        ),
        in_specs=[pl.BlockSpec(memory_space=pl.ANY)] * 6,
        out_specs=(pl.BlockSpec(memory_space=pl.ANY),) * 2,
        scratch_shapes=[
            pltpu.VMEM((STEPS + 1, BLOCKS, LAYERS, ROWS, LANES), f32),
            pltpu.VMEM((STEPS, 3, LAYERS, ROWS, BLOCKS * LANES), jnp.bfloat16),
            pltpu.VMEM((STEPS, 2, BLOCKS, ROWS, LANES), f32),
            pltpu.VMEM((STEPS, 2, BLOCKS, ROWS, LANES), f32),
            pltpu.VMEM((STEPS, 2, CHUNKS, 2 * LAYERS, LANES), f32),
            pltpu.VMEM((STEPS, 2, CHUNKS, 2 * LAYERS, LANES), f32),
            pltpu.VMEM((STEPS, BLOCKS, ROWS, LANES), f32),
            pltpu.VMEM((BLOCKS, ROWS, LANES), f32),
            pltpu.VMEM((PROWS, LANES), f32),
            pltpu.VMEM((PROWS, LANES), jnp.int32),
            pltpu.VMEM((STEPS, PROWS, LANES), f32),
            pltpu.VMEM((STEPS + 1, PZ, PROWS, LANES), f32),
            pltpu.VMEM((STEPS, PZ, PROWS, LANES), f32),
            pltpu.VMEM((STEPS, PZ, PROWS, LANES), jnp.int32),
            pltpu.VMEM((STEPS + 1, 2, PZ, LANES), f32),
            pltpu.VMEM((STEPS, 2, PZ, LANES), f32),
            pltpu.VMEM((STEPS, 8, LANES), f32),
            pltpu.VMEM((STEPS, 2, 8, LANES), f32),
            pltpu.VMEM((LAYERS, ROWS, LANES), f32),
            dma((BLOCKS,)),
            dma((STEPS, 3)),
            dma((2,)),
            dma((STEPS, 2)),
            dma((CHUNKS + 1,)),
            dma((STEPS, 2, CHUNKS)),
            dma((STEPS, 2, CHUNKS)),
            dma((STEPS, 2, CHUNKS)),
            dma((STEPS, 2, CHUNKS)),
            dma((STEPS,)),
            dma((STEPS, CHUNKS)),
            dma((1,)),
            dma((CHUNKS,)),
            dma((STEPS, BLOCKS, 2)),
            dma((STEPS,)),
            dma((STEPS, 2)),
            dma((STEPS, 2)),
            dma((STEPS, 2)),
            dma((STEPS, 2)),
        ],
        compiler_params=pltpu.CompilerParams(
            collective_id=0, has_side_effects=True, vmem_limit_bytes=48 * 1024 * 1024
        ),
        cost_estimate=pl.CostEstimate(flops=35_000_000, bytes_accessed=11_000_000, transcendentals=0),
    )(seed_fluid, seed_plate, velocity, enthalpy, phase, contact)


def solution(mesh):
    return jax.shard_map(
        on_device,
        mesh=mesh,
        in_specs=(
            P("ty", "tx", None),
            P(None, "ty", "tx"),
            P(None, None, "ty", "tx", None),
            P(None, None, "ty", "tx"),
            P(None, None, "ty", "tx"),
            P("ty", "tx"),
        ),
        out_specs=(P("ty", "tx", None), P(None, "ty", "tx")),
        check_vma=False,
    )
```

time: 616 us -> 52.9 us (0.09); the launches traced: 605 us -> 52.5 us
  waiting for transfers between devices: 225 us -> 0 us
  starting transfers between devices: 153 us -> 0 us
  other arithmetic: 99.7 us -> 0 us
  blocking collectives: 86.9 us -> 0 us
  Pallas kernels: 0 us -> 44.9 us
  local copies, waits for them, and re-layouts: 26.2 us -> 7.01 us
  between operations: 14.9 us -> 0.65 us
    reduce_scatter x4 -> x0, waiting for transfers between devices: 191 us -> none  [to_plate(): lax.psum_scatter(jnp.where(is_owner, spread, 0.0), 'ty', scatter_dimensio...]
    ppermute x32 -> x0, starting transfers between devices: 94.2 us -> none  [the longest x16 50 us: with_halo(): lax.ppermute(lax.slice_in_dim(block, block.shape[dim] - width, None, axis...]
    all_gather x4 -> x0, blocking collectives: 86.9 us -> none  [on_device(): returned = lax.all_gather(coupling, 'ty', axis=0, tiled=True)]
    all_to_all x8 -> x0, starting transfers between devices: 58.2 us -> none  [the longest x4 29.2 us: on_device(): lax.all_to_all(returned, 'tx', split_axis=0, concat_axis=1, tiled=True)]
    pallas_call x0 -> x1, Pallas kernels: none -> 44.9 us  [on_device(): pl.pallas_call(kernel, out_shape=(jax.ShapeDtypeStruct(seed_fluid.shape,...]
    ppermute x32 -> x0, waiting for transfers between devices: 29.4 us -> none  [the longest x16 20.6 us: with_halo(): lax.ppermute(lax.slice_in_dim(block, block.shape[dim] - width, None, axis...]
    slice x12 -> x0, other arithmetic: 22.3 us -> none  [the longest x8 18.2 us: with_halo(): lax.slice_in_dim(block, block.shape[dim] - width, None, axis=dim)]
    concatenate x4 -> x0, other arithmetic: 20.3 us -> none  [with_halo(): block = jnp.concatenate([low, block, high], axis=dim)]
  transfers between devices with their start and end apart: 44 -> 0, of which waited for: 12 -> 0; matrix products, arithmetic and copies ran while one was open for 18% -> 0% of each run, Pallas kernels for 0% -> 0%
where the time goes in v1:
time: 52.9 us; the launch traced here: 52.5 us
  Pallas kernels  44.9 us (85%)
  local copies, waits for them, and re-layouts  7.01 us (13%)
  between operations  0.65 us (1%)
    pallas_call x1, Pallas kernels, on_device(): pl.pallas_call(kernel, out_shape=(jax.ShapeDtypeStruct(seed_fluid.shape,...  44.9 us
    unnamed x12, local copies, waits for them, and re-layouts  7.01 us

profile of v1, /device:TPU:6, one launch (start us, length us, event | category | flops | bytes accessed | tf_op | source)
XLA Modules:
  0.0 52.5 jit_solution(17163525268848247026)
XLA Ops:
  0.6 0.0 copy-start
  0.6 1.2 %copy-done = f32[4,64,1024]{2,1,0:T(8,128)S(1)} copy-done((f32[4,64,1024]{2,1,0:T(8,128)S(1)}, f32[4,64,1024]{2,1,0:T(8,128)}, u32[]{:S(2)}) %copy-start) | copy-done | bytes 1048600
  1.9 0.0 copy-start.1
  1.9 1.2 %copy-done.1 = f32[4,16,32,128]{3,2,1,0:T(8,128)S(1)} copy-done((f32[4,16,32,128]{3,2,1,0:T(8,128)S(1)}, f32[4,16,32,128]{3,2,1,0:T(8,128)}, u32[]{:S(2)}) %copy-start.1) | copy-done | bytes 1048600
  3.1 0.0 copy-start.2
  3.1 1.2 %copy-done.2 = s32[4,16,32,128]{3,2,1,0:T(8,128)S(1)} copy-done((s32[4,16,32,128]{3,2,1,0:T(8,128)S(1)}, s32[4,16,32,128]{3,2,1,0:T(8,128)}, u32[]{:S(2)}) %copy-start.2) | copy-done | bytes 1048600
  4.3 0.0 copy-start.3
  4.3 0.9 %copy-done.3 = f32[16,32,128]{2,1,0:T(8,128)S(1)} copy-done((f32[16,32,128]{2,1,0:T(8,128)S(1)}, f32[16,32,128]{2,1,0:T(8,128)}, u32[]{:S(2)}) %copy-start.3) | copy-done | bytes 262168
  5.3 0.0 copy-start.4
  5.3 0.7 %copy-done.4 = s32[32,128]{1,0:T(8,128)S(1)} copy-done((s32[32,128]{1,0:T(8,128)S(1)}, s32[32,128]{1,0:T(8,128)}, u32[]{:S(2)}) %copy-start.4) | copy-done | bytes 16408
  6.0 44.9 %shard_map.77 = (f32[4,64,1024]{2,1,0:T(8,128)S(1)}, f32[16,32,128]{2,1,0:T(8,128)S(1)}) custom-call(f32[4,64,1024]{2,1,0:T(8,128)S(1)} %copy-done, f32[16,32,128]{2,1,0:T(8,128)S(1)} %copy-done.3, bf16[4,3,4,64,1024]{4,3,2,1,0:T(8,128)(2,1)} %velocity.1, f32[4,16,32,128]{3,2,1,0:T(8,128)S(1)} %copy-done.1, s32[4,16,32,128]{3,2,1,0:T(8,128)S(1)} %copy-done.2, ...), custom_call_target="tpu_custom_call" | custom-call | flops 35000000 | bytes 11000000 | tf_op jit(solution)/shard_map/pallas_call | solution.py:440
  50.9 1.0 %copy.10 = f32[4,64,1024]{2,1,0:T(8,128)} copy(f32[4,64,1024]{2,1,0:T(8,128)S(1)} %get-tuple-element.4) | data formatting | bytes 2097152
  51.8 0.7 %copy.11 = f32[16,32,128]{2,1,0:T(8,128)} copy(f32[16,32,128]{2,1,0:T(8,128)S(1)} %get-tuple-element.5) | data formatting | bytes 524288
Async XLA Ops:
  0.6 1.2 %copy-start = (f32[4,64,1024]{2,1,0:T(8,128)S(1)}, f32[4,64,1024]{2,1,0:T(8,128)}, u32[]{:S(2)}) copy-start(f32[4,64,1024]{2,1,0:T(8,128)} %seed_fluid.1) | copy-start | bytes 3145732
  1.9 1.2 %copy-start.1 = (f32[4,16,32,128]{3,2,1,0:T(8,128)S(1)}, f32[4,16,32,128]{3,2,1,0:T(8,128)}, u32[]{:S(2)}) copy-start(f32[4,16,32,128]{3,2,1,0:T(8,128)} %enthalpy.1) | copy-start | bytes 3145732
  3.1 1.2 %copy-start.2 = (s32[4,16,32,128]{3,2,1,0:T(8,128)S(1)}, s32[4,16,32,128]{3,2,1,0:T(8,128)}, u32[]{:S(2)}) copy-start(s32[4,16,32,128]{3,2,1,0:T(8,128)} %phase.1) | copy-start | bytes 3145732
  4.3 0.9 %copy-start.3 = (f32[16,32,128]{2,1,0:T(8,128)S(1)}, f32[16,32,128]{2,1,0:T(8,128)}, u32[]{:S(2)}) copy-start(f32[16,32,128]{2,1,0:T(8,128)} %seed_plate.1) | copy-start | bytes 786436
  5.3 0.7 %copy-start.4 = (s32[32,128]{1,0:T(8,128)S(1)}, s32[32,128]{1,0:T(8,128)}, u32[]{:S(2)}) copy-start(s32[32,128]{1,0:T(8,128)} %contact.1) | copy-start | bytes 49156

commit v2 on v1

v2 whole, which is shorter than its diff:
```python
import jax
import jax.numpy as jnp
from jax import lax
from jax.experimental import pallas as pl
from jax.experimental.pallas import tpu as pltpu
from jax.sharding import PartitionSpec as P

MESH = pl.DeviceIdType.MESH
STEPS = 4
PZ = 16
LAYERS = 4
ROWS = 64
BLOCKS = 8
CHUNKS = 4
PROWS = 32
LANES = 128
PLATE_SLOTS = ((0, 5), (1, 8), (2, 11), (3, 15))
CARRY_SLOTS = ((1, 8), (2, 12), (3, 15))
COUPLE_SLOTS = ((0, 5), (1, 10), (2, 12), (3, 15))
TX = 8
TY = 16


def kernel(
    seed_fluid, seed_plate, velocity, enthalpy, phase, contact,
    out_fluid, out_plate,
    F, NF, V, ZS, ZR, YS, YR, CR, CC, CF, CI, PR, PT, NP, TOP, EN, PH, SL, PYS, PYR, PXS, PXR, SXM, SXP, AS, AM, CP, D, ND, DXM, DXP, DYS, DYR,
    load_f, load_v, load_p, load_e, out_sem,
    zs_sem, zr_sem, ys_sem, yr_sem, cs_sem, cr_sem, ccs_sem, ccr_sem, fs_sem, pr_sem,
    pys_sem, pyr_sem, pxs_sem, pxr_sem, dys_sem, dyr_sem,
):
    tx = lax.axis_index("tx")
    ty = lax.axis_index("ty")
    has_down, has_up = ty > 0, ty < TY - 1
    has_lo, has_hi = tx > 0, tx < TX - 1
    is_wall = ty == 0
    home_tx = ty // 2
    is_self = (tx == 0) & (ty == 0)
    not_self = jnp.logical_not(is_self)
    lane = lax.broadcasted_iota(jnp.int32, (ROWS, LANES), 1)
    row = lax.broadcasted_iota(jnp.int32, (ROWS, LANES), 0)

    def lanes(b):
        return pl.ds(pl.multiple_of(b * LANES, LANES), LANES)

    f_loads = [
        pltpu.make_async_copy(seed_fluid.at[:, :, pl.ds(b * LANES, LANES)], F.at[b], load_f.at[b])
        for b in range(BLOCKS)
    ]
    for copy in f_loads:
        copy.start()
    for c in (2, 1, 0):
        pltpu.make_async_copy(velocity.at[STEPS - 1, c], V.at[STEPS - 1, c], load_v.at[STEPS - 1, c]).start()
    contact_load = pltpu.make_async_copy(contact, CI, load_p.at[1])
    contact_load.start()
    plate_load = pltpu.make_async_copy(seed_plate, PT, load_p.at[0])
    plate_load.start()

    def late_loads(n):
        e = pltpu.make_async_copy(enthalpy.at[n], EN.at[n], load_e.at[n, 0])
        p = pltpu.make_async_copy(phase.at[n], PH.at[n], load_e.at[n, 1])
        v = [pltpu.make_async_copy(velocity.at[n, c], V.at[n, c], load_v.at[n, c]) for c in range(3)]
        return e, p, v

    barrier = pltpu.get_barrier_semaphore()

    def greet(cond, device):
        @pl.when(cond)
        def _():
            pl.semaphore_signal(barrier, inc=1, device_id=device, device_id_type=MESH)

        return jnp.where(cond, 1, 0)

    expected = greet(not_self, (home_tx, 0))
    expected += greet(has_lo, (tx - 1, ty))
    expected += greet(has_hi, (tx + 1, ty))
    expected += greet(has_down, (tx, ty - 1))
    expected += greet(has_up, (tx, ty + 1))

    @pl.when(is_wall)
    def _():
        for c in range(TX):
            for r in range(2):
                greet((tx > 0) | (2 * c + r > 0), (c, 2 * tx + r))

    expected += jnp.where(is_wall, jnp.where(is_self, 15, 16), 0)

    for n in (3, 2, 1, 0):
        e, p, v = late_loads(n)
        e.start()
        p.start()
        if n < STEPS - 1:
            for copy in v:
                copy.start()

    def remote(src, dst, send, recv, device):
        return pltpu.make_async_remote_copy(
            src_ref=src, dst_ref=dst, send_sem=send, recv_sem=recv, device_id=device, device_id_type=MESH
        )

    def z_down(s, j):
        blocks = pl.ds(2 * j, 2)
        return remote(ZS.at[s, 0, blocks], ZR.at[s, 1, blocks], zs_sem.at[s, 0, j], zr_sem.at[s, 1, j], (tx, ty - 1))

    def z_up(s, j):
        blocks = pl.ds(2 * j, 2)
        return remote(ZS.at[s, 1, blocks], ZR.at[s, 0, blocks], zs_sem.at[s, 1, j], zr_sem.at[s, 0, j], (tx, ty + 1))

    def y_lo(s, j):
        return remote(YS.at[s, 0, j], YR.at[s, 1, j], ys_sem.at[s, 0, j], yr_sem.at[s, 1, j], (tx - 1, ty))

    def y_hi(s, j):
        return remote(YS.at[s, 1, j], YR.at[s, 0, j], ys_sem.at[s, 1, j], yr_sem.at[s, 0, j], (tx + 1, ty))

    def wall_out(s, j, bb, r):
        b = 2 * j + bb
        return remote(
            AM.at[s, b, pl.ds(PROWS * r, PROWS)], PR.at[s], fs_sem.at[s, b, r], pr_sem.at[s], (b, 2 * tx + r)
        )

    def each_wall_out(s, j, act):
        for bb in range(2):
            for r in range(2):
                away = is_wall if (bb, r) != (0, 0) else is_wall & ((tx > 0) | (j > 0))

                @pl.when(away)
                def _(bb=bb, r=r):
                    act(wall_out(s, j, bb, r))

    def launch_y(s, j):
        pl.when(has_lo)(lambda: y_lo(s, j).start())
        pl.when(has_hi)(lambda: y_hi(s, j).start())

    def launch_z(s, j):
        pl.when(has_down)(lambda: z_down(s, j).start())
        pl.when(has_up)(lambda: z_up(s, j).start())

    def wall_launch(s, j):
        each_wall_out(s, j, lambda copy: copy.start())

        @pl.when(is_self & (j == 0))
        def _():
            pltpu.make_async_copy(AM.at[s, 0, pl.ds(0, PROWS)], PR.at[s], pr_sem.at[s]).start()

    def sent(s, j):
        pl.when(has_lo)(lambda: y_lo(s, j).wait_send())
        pl.when(has_hi)(lambda: y_hi(s, j).wait_send())
        pl.when(has_down)(lambda: z_down(s, j).wait_send())
        pl.when(has_up)(lambda: z_up(s, j).wait_send())

    def stage_z(s, j):
        n = STEPS - 1 - s
        for bb in range(2):
            b = 2 * j + bb
            g = 0.1 * F[b, 0]
            ZS[s, 0, b] = g + g * V[n, 2, 0, :, lanes(b)].astype(jnp.float32)
            g = 0.1 * F[b, LAYERS - 1]
            ZS[s, 1, b] = g - g * V[n, 2, LAYERS - 1, :, lanes(b)].astype(jnp.float32)

    def stage_y(s, j, field, out):
        n = STEPS - 1 - s
        for q in range(2 * LAYERS):
            b, l = 2 * j + q // LAYERS, q % LAYERS
            g = 0.1 * field[b, l, 0:1, :]
            v = V[n, 1, l, 0:16, lanes(b)].astype(jnp.float32)[0:1]
            out[s, 0, j, q : q + 1, :] = g + g * v
            g = 0.1 * field[b, l, ROWS - 1 : ROWS, :]
            v = V[n, 1, l, ROWS - 16 : ROWS, lanes(b)].astype(jnp.float32)[15:16]
            out[s, 1, j, q : q + 1, :] = g - g * v

    def prime(s, field, xp, xm):
        for l in range(LAYERS):
            g = 0.1 * field[0, l]
            xp[l] = pltpu.roll(g + g * V[STEPS - 1 - s, 0, l, :, lanes(0)].astype(jnp.float32), LANES - 1, 1)
            xm[l] = jnp.zeros((ROWS, LANES), jnp.float32)

    def interior(s, b, field, out, xp, xm):
        n = STEPS - 1 - s
        after = jnp.minimum(b + 1, BLOCKS - 1)
        weight = jnp.where(b < BLOCKS - 1, 0.1, 0.0)
        pending = below = None
        for l in range(LAYERS):
            f = field[b, l]
            g = 0.1 * f
            gu = g * V[n, 0, l, :, lanes(b)].astype(jnp.float32)
            gv = g * V[n, 1, l, :, lanes(b)].astype(jnp.float32)
            gw = g * V[n, 2, l, :, lanes(b)].astype(jnp.float32)
            beyond = weight * field[after, l]
            beyond = beyond + beyond * V[n, 0, l, :, lanes(after)].astype(jnp.float32)
            from_beyond = pltpu.roll(beyond, LANES - 1, 1)
            from_left = pltpu.roll(g - gu, 1, 1)
            from_above = pltpu.roll(g + gv, ROWS - 1, 0)
            from_below = pltpu.roll(g - gv, 1, 0)
            total = 0.4 * f
            total += jnp.where(lane == LANES - 1, from_beyond, xp[l])
            total += jnp.where(lane == 0, xm[l], from_left)
            total += jnp.where(row == ROWS - 1, 0.0, from_above)
            total += jnp.where(row == 0, 0.0, from_below)
            xp[l] = from_beyond
            xm[l] = from_left
            if l > 0:
                out[b, l - 1] = pending + (g + gw)
                total += below
            below = g - gw
            pending = total
        out[b, LAYERS - 1] = pending

    def finish(s, j):
        @pl.when(has_lo)
        def _():
            y_hi(s, j).wait_recv()
            for q in range(2 * LAYERS):
                b, l = 2 * j + q // LAYERS, q % LAYERS
                NF[b, l, 0:1, :] += YR[s, 0, j, q : q + 1, :]

        @pl.when(has_hi)
        def _():
            y_lo(s, j).wait_recv()
            for q in range(2 * LAYERS):
                b, l = 2 * j + q // LAYERS, q % LAYERS
                NF[b, l, ROWS - 1 : ROWS, :] += YR[s, 1, j, q : q + 1, :]

        for bb in range(2):
            for l in range(1, LAYERS - 1):
                F[2 * j + bb, l] = NF[2 * j + bb, l]

        @pl.when(has_down)
        def _():
            z_up(s, j).wait_recv()
            for bb in range(2):
                F[2 * j + bb, 0] = NF[2 * j + bb, 0] + ZR[s, 0, 2 * j + bb]

        @pl.when(has_up)
        def _():
            z_down(s, j).wait_recv()
            for bb in range(2):
                F[2 * j + bb, LAYERS - 1] = NF[2 * j + bb, LAYERS - 1] + ZR[s, 1, 2 * j + bb]

        @pl.when(ty == TY - 1)
        def _():
            for bb in range(2):
                F[2 * j + bb, LAYERS - 1] = NF[2 * j + bb, LAYERS - 1]

        @pl.when(is_wall)
        def _():
            for bb in range(2):
                F[2 * j + bb, 0] = NF[2 * j + bb, 0]

            @pl.when(s < STEPS - 1)
            def _():
                for bb in range(2):
                    AS[s + 1, 2 * j + bb] = NF[2 * j + bb, 0]

            @pl.when(s == 0)
            def _():
                for bb in range(2):
                    AM[1, 2 * j + bb] = NF[2 * j + bb, 0]
                wall_launch(1, j)

    def d_lo(s):
        return remote(DYS.at[s, 0], DYR.at[s, 1], dys_sem.at[s, 0], dyr_sem.at[s, 1], (tx - 1, ty))

    def d_hi(s):
        return remote(DYS.at[s, 1], DYR.at[s, 0], dys_sem.at[s, 1], dyr_sem.at[s, 0], (tx + 1, ty))

    def carry_on(s):
        prime(s, D, DXP, DXM)

        def body(b, c):
            interior(s, b, D, ND, DXP, DXM)
            return c

        lax.fori_loop(0, BLOCKS, body, 0)
        for here, copy, side, at in ((has_lo, d_hi, 0, 0), (has_hi, d_lo, 1, ROWS - 1)):
            @pl.when(here)
            def _(copy=copy, side=side, at=at):
                copy(s).wait_recv()
                for b in range(BLOCKS):
                    for l in range(LAYERS):
                        q = LAYERS * (b % 2) + l
                        ND[b, l, at : at + 1, :] += DYR[s, side, b // 2, q : q + 1, :]

        pl.when(has_lo)(lambda: d_lo(s).wait_send())
        pl.when(has_hi)(lambda: d_hi(s).wait_send())

        @pl.when(s < STEPS - 1)
        def _():
            for b in range(BLOCKS):
                AM[s + 1, b] = AS[s + 1, b] + ND[b, 0]

            def body(j, c):
                wall_launch(s + 1, j)
                return c

            lax.fori_loop(0, CHUNKS, body, 0)

    def couple(s):
        for j in range(CHUNKS):
            blocks = pl.ds(2 * j, 2)
            pltpu.make_async_copy(CR.at[s, blocks], CR.at[s, blocks], cr_sem.at[s, j]).wait()

        @pl.when(s == 0)
        def _():
            for j in range(CHUNKS):
                blocks = pl.ds(2 * j, 2)
                pltpu.make_async_copy(CC.at[blocks], CC.at[blocks], ccr_sem.at[j]).wait()

        def body(b, c):
            wall = AS[s, b] + D[b, 0]
            D[b, 0] = ND[b, 0] + CC[b] * (0.5 * CR[s, b] - 0.5 * wall)
            for l in range(1, LAYERS):
                D[b, l] = ND[b, l]
            return c

        lax.fori_loop(0, BLOCKS, body, 0)

        @pl.when(s < STEPS - 1)
        def _():
            def body(j, c):
                stage_y(s + 1, j, D, DYS)
                return c

            lax.fori_loop(0, CHUNKS, body, 0)
            pl.when(has_lo)(lambda: d_lo(s + 1).start())
            pl.when(has_hi)(lambda: d_hi(s + 1).start())

        @pl.when(s == STEPS - 1)
        def _():
            def body(b, c):
                for l in range(LAYERS):
                    F[b, l] += D[b, l]
                return c

            lax.fori_loop(0, BLOCKS, body, 0)
            for j in range(CHUNKS):
                put_out(j)

    def put_out(j):
        for bb in range(2):
            b = 2 * j + bb
            pltpu.make_async_copy(F.at[b], out_fluid.at[:, :, lanes(b)], out_sem.at[j]).start()

    tile_rows = pl.ds(pl.multiple_of(PROWS * lax.rem(ty, 2), PROWS), PROWS)
    tile_chunk = tx // 2

    def wall_in(s):
        return remote(TOP.at[s], CR.at[s, tx, tile_rows], cs_sem.at[s], cr_sem.at[s, tile_chunk], (home_tx, 0))

    def contact_in():
        return remote(CF, CC.at[tx, tile_rows], ccs_sem.at[0], ccr_sem.at[tile_chunk], (home_tx, 0))

    def py_lo(s):
        return remote(PYS.at[s, 0], PYR.at[s, 1], pys_sem.at[s, 0], pyr_sem.at[s, 1], (tx, ty - 1))

    def py_hi(s):
        return remote(PYS.at[s, 1], PYR.at[s, 0], pys_sem.at[s, 1], pyr_sem.at[s, 0], (tx, ty + 1))

    def px_lo(s):
        return remote(PXS.at[s], PXR.at[s, 1], pxs_sem.at[s, 0], pxr_sem.at[s, 1], (tx - 1, ty))

    def px_hi(s):
        return remote(PXS.at[s], PXR.at[s, 0], pxs_sem.at[s, 1], pxr_sem.at[s, 0], (tx + 1, ty))

    def wall_reply(s):
        pl.when(not_self)(lambda: wall_in(s).start())

        @pl.when(is_self)
        def _():
            pltpu.make_async_copy(TOP.at[s], CR.at[s, 0, pl.ds(0, PROWS)], cr_sem.at[s, 0]).start()

    def plate_launch(s):
        pl.when(has_lo)(lambda: px_lo(s).start())
        pl.when(has_hi)(lambda: px_hi(s).start())
        pl.when(has_down)(lambda: py_lo(s).start())
        pl.when(has_up)(lambda: py_hi(s).start())

    def plate_sent(s):
        pl.when(not_self)(lambda: wall_in(s).wait_send())
        pl.when(has_lo)(lambda: px_lo(s).wait_send())
        pl.when(has_hi)(lambda: px_hi(s).wait_send())
        pl.when(has_down)(lambda: py_lo(s).wait_send())
        pl.when(has_up)(lambda: py_hi(s).wait_send())

    small_lane = lax.broadcasted_iota(jnp.int32, (8, LANES), 1)

    def edge_rows(s, z, value):
        PYS[s, 0, z : z + 1, :] = value[0:1]
        PYS[s, 1, z : z + 1, :] = value[PROWS - 1 : PROWS]

    def edge_columns(packed, z, value):
        for k in range(PROWS // 8):
            place = 2 * (16 * k + z)
            part = pltpu.roll(value[8 * k : 8 * k + 8], place + 1, 1)
            packed = jnp.where((small_lane == place) | (small_lane == place + 1), part, packed)
        return packed

    def merge(parts):
        while len(parts) > 1:
            parts = [x + y for x, y in zip(parts[::2], parts[1::2])]
        return parts[0]

    def plate_edges(s, plate):
        parts = []
        for z in range(PZ):
            value = plate[z]
            edge_rows(s, z, value)
            parts.append(edge_columns(jnp.zeros((8, LANES), jnp.float32), z, value))
        PXS[s] = merge(parts)

    plate_lane = lax.broadcasted_iota(jnp.int32, (PROWS, LANES), 1)
    plate_row = lax.broadcasted_iota(jnp.int32, (PROWS, LANES), 0)

    def slopes_of(n):
        e, p, _ = late_loads(n)
        e.wait()
        p.wait()
        for z in range(PZ):
            saved, state = EN[n, z], PH[n, z]
            slopes = 1.0 / (1.0 + 8.0 * saved * (1.0 - saved))
            SL[z] = jnp.where(state == 0, 1.0, jnp.where(state == 2, 0.7, slopes))

    def plate_step(s):
        @pl.when(s > 0)
        def _():
            for z in range(PZ):
                PT[z] = NP[z]

        pl.when(has_lo)(lambda: px_hi(s).wait_recv())
        pl.when(has_hi)(lambda: px_lo(s).wait_recv())
        pl.when(has_down)(lambda: py_hi(s).wait_recv())
        pl.when(has_up)(lambda: py_lo(s).wait_recv())
        beside = jnp.where(
            small_lane % 2 == 0, pltpu.roll(PXR[s, 1], LANES - 1, 1), pltpu.roll(PXR[s, 0], 1, 1)
        )
        for z in range(PZ):
            value = PT[z]
            ends = [pltpu.roll(beside, LANES - 1 - 2 * (16 * k + z), 1) for k in range(PROWS // 8)]
            ends = jnp.concatenate(ends, 0)
            total = jnp.where(plate_lane == 0, ends, pltpu.roll(value, 1, 1))
            total += jnp.where(plate_lane == LANES - 1, ends, pltpu.roll(value, LANES - 1, 1))
            total += jnp.where(plate_row == 0, PYR[s, 0, z : z + 1, :], pltpu.roll(value, 1, 0))
            total += jnp.where(plate_row == PROWS - 1, PYR[s, 1, z : z + 1, :], pltpu.roll(value, PROWS - 1, 0))
            if z > 0:
                total += PT[z - 1]
            if z < PZ - 1:
                total += PT[z + 1]
            NP[z] = value + SL[z] * (0.12 * (total - 6.0 * value))

    def plate_top(s):
        pltpu.make_async_copy(PR.at[s], PR.at[s], pr_sem.at[s]).wait()
        wall = PR[s] + jnp.where(s > 0, CP[...], 0.0)
        coupling = CF[...] * (0.5 * PT[PZ - 1] - 0.5 * wall)
        CP[...] = coupling
        value = NP[PZ - 1] - SL[PZ - 1] * coupling
        NP[PZ - 1] = value

        @pl.when(s < STEPS - 1)
        def _():
            TOP[s + 1] = value
            wall_reply(s + 1)
            plate_edges(s + 1, NP)
            plate_launch(s + 1)

        plate_sent(s)

        @pl.when(s < STEPS - 1)
        def _():
            slopes_of(STEPS - 2 - s)

        @pl.when(s == STEPS - 1)
        def _():
            pltpu.make_async_copy(NP, out_plate, out_sem.at[CHUNKS]).start()

    for absent, side in ((ty == 0, 0), (ty == TY - 1, 1)):
        @pl.when(absent)
        def _(side=side):
            for s in range(STEPS):
                PYR[s, side] = jnp.zeros((PZ, LANES), jnp.float32)

    for absent, side in ((tx == 0, 0), (tx == TX - 1, 1)):
        @pl.when(absent)
        def _(side=side):
            for s in range(STEPS):
                PXR[s, side] = jnp.zeros((8, LANES), jnp.float32)

    contact_load.wait()
    CF[...] = CI[...].astype(jnp.float32)
    for copy in f_loads:
        copy.wait()
    for c in (2, 1, 0):
        pltpu.make_async_copy(velocity.at[STEPS - 1, c], V.at[STEPS - 1, c], load_v.at[STEPS - 1, c]).wait()

    def first_stage(j, carry):
        stage_z(0, j)
        stage_y(0, j, F, YS)
        return carry

    lax.fori_loop(0, CHUNKS, first_stage, 0)

    @pl.when(is_wall)
    def _():
        for b in range(BLOCKS):
            AS[0, b] = F[b, 0]
            AM[0, b] = F[b, 0]
            for l in range(LAYERS):
                D[b, l] = jnp.zeros((ROWS, LANES), jnp.float32)
                ND[b, l] = jnp.zeros((ROWS, LANES), jnp.float32)

    plate_load.wait()
    TOP[0] = PT[PZ - 1]
    plate_edges(0, PT)
    pl.semaphore_wait(barrier, expected)

    def first_wall(chunk):
        @pl.when(tile_chunk == chunk)
        def _():
            wall_reply(0)
            pl.when(not_self)(lambda: contact_in().start())

            @pl.when(is_self)
            def _():
                pltpu.make_async_copy(CF, CC.at[0, pl.ds(0, PROWS)], ccr_sem.at[0]).start()

    first_wall(0)

    @pl.when(is_wall)
    def _():
        def body(j, carry):
            wall_launch(0, j)
            return carry

        lax.fori_loop(0, CHUNKS, body, 0)

    def first_launch(j, carry):
        launch_y(0, j)
        launch_z(0, j)
        return carry

    lax.fori_loop(0, CHUNKS, first_launch, 0)
    first_wall(1)
    plate_launch(0)

    def first_interior(b, carry):
        interior(0, b, F, NF, SXP, SXM)
        return carry

    prime(0, F, SXP, SXM)
    lax.fori_loop(0, BLOCKS // 2, first_interior, 0)
    first_wall(2)
    lax.fori_loop(BLOCKS // 2, BLOCKS, first_interior, 0)
    first_wall(3)
    slopes_of(STEPS - 1)

    def at(t, slots, act):
        due, s = False, 0
        for step, place in slots:
            due, s = due | (t == place), jnp.where(t == place, step, s)
        pl.when(due)(lambda: act(s))

    def plate(s):
        plate_step(s)
        plate_top(s)

    def slot(t, carry):
        s, j = t // CHUNKS, lax.rem(t, CHUNKS)
        finish(s, j)

        @pl.when(s < STEPS - 1)
        def _():
            @pl.when(j == 0)
            def _():
                for copy in late_loads(STEPS - 2 - s)[2]:
                    copy.wait()

            stage_z(s + 1, j)
            launch_z(s + 1, j)
            stage_y(s + 1, j, F, YS)
            launch_y(s + 1, j)

            @pl.when(j == 0)
            def _():
                prime(s + 1, F, SXP, SXM)

            def body(b, c):
                interior(s + 1, b, F, NF, SXP, SXM)
                return c

            lax.fori_loop(jnp.maximum(2 * j - 1, 0), jnp.where(j == CHUNKS - 1, BLOCKS, 2 * j + 1), body, 0)

        pl.when((s == STEPS - 1) & (ty > 0))(lambda: put_out(j))
        sent(s, j)

        @pl.when(is_wall)
        def _():
            at(t, CARRY_SLOTS, carry_on)
            at(t, COUPLE_SLOTS, couple)

        at(t, PLATE_SLOTS, plate)
        return carry

    lax.fori_loop(0, STEPS * CHUNKS, slot, 0)

    @pl.when(is_wall)
    def _():
        def body(t, c):
            each_wall_out(t // CHUNKS, lax.rem(t, CHUNKS), lambda copy: copy.wait_send())
            return c

        lax.fori_loop(0, STEPS * CHUNKS, body, 0)

    pl.when(not_self)(lambda: contact_in().wait_send())
    for j in range(CHUNKS):
        pltpu.make_async_copy(F.at[pl.ds(2 * j, 2)], F.at[pl.ds(2 * j, 2)], out_sem.at[j]).wait()
    pltpu.make_async_copy(NP, out_plate, out_sem.at[CHUNKS]).wait()


def on_device(seed_fluid, seed_plate, velocity, enthalpy, phase, contact):
    f32 = jnp.float32
    dma = pltpu.SemaphoreType.DMA
    return pl.pallas_call(
        kernel,
        out_shape=(
            jax.ShapeDtypeStruct(seed_fluid.shape, f32),
            jax.ShapeDtypeStruct(seed_plate.shape, f32),
        ),
        in_specs=[pl.BlockSpec(memory_space=pl.ANY)] * 6,
        out_specs=(pl.BlockSpec(memory_space=pl.ANY),) * 2,
        scratch_shapes=[
            pltpu.VMEM((BLOCKS, LAYERS, ROWS, LANES), f32),
            pltpu.VMEM((BLOCKS, LAYERS, ROWS, LANES), f32),
            pltpu.VMEM((STEPS, 3, LAYERS, ROWS, BLOCKS * LANES), jnp.bfloat16),
            pltpu.VMEM((STEPS, 2, BLOCKS, ROWS, LANES), f32),
            pltpu.VMEM((STEPS, 2, BLOCKS, ROWS, LANES), f32),
            pltpu.VMEM((STEPS, 2, CHUNKS, 2 * LAYERS, LANES), f32),
            pltpu.VMEM((STEPS, 2, CHUNKS, 2 * LAYERS, LANES), f32),
            pltpu.VMEM((STEPS, BLOCKS, ROWS, LANES), f32),
            pltpu.VMEM((BLOCKS, ROWS, LANES), f32),
            pltpu.VMEM((PROWS, LANES), f32),
            pltpu.VMEM((PROWS, LANES), jnp.int32),
            pltpu.VMEM((STEPS, PROWS, LANES), f32),
            pltpu.VMEM((PZ, PROWS, LANES), f32),
            pltpu.VMEM((PZ, PROWS, LANES), f32),
            pltpu.VMEM((STEPS, PROWS, LANES), f32),
            pltpu.VMEM((STEPS, PZ, PROWS, LANES), f32),
            pltpu.VMEM((STEPS, PZ, PROWS, LANES), jnp.int32),
            pltpu.VMEM((PZ, PROWS, LANES), f32),
            pltpu.VMEM((STEPS + 1, 2, PZ, LANES), f32),
            pltpu.VMEM((STEPS, 2, PZ, LANES), f32),
            pltpu.VMEM((STEPS + 1, 8, LANES), f32),
            pltpu.VMEM((STEPS, 2, 8, LANES), f32),
            pltpu.VMEM((LAYERS, ROWS, LANES), f32),
            pltpu.VMEM((LAYERS, ROWS, LANES), f32),
            pltpu.VMEM((STEPS, BLOCKS, ROWS, LANES), f32),
            pltpu.VMEM((STEPS, BLOCKS, ROWS, LANES), f32),
            pltpu.VMEM((PROWS, LANES), f32),
            pltpu.VMEM((BLOCKS, LAYERS, ROWS, LANES), f32),
            pltpu.VMEM((BLOCKS, LAYERS, ROWS, LANES), f32),
            pltpu.VMEM((LAYERS, ROWS, LANES), f32),
            pltpu.VMEM((LAYERS, ROWS, LANES), f32),
            pltpu.VMEM((STEPS, 2, CHUNKS, 2 * LAYERS, LANES), f32),
            pltpu.VMEM((STEPS, 2, CHUNKS, 2 * LAYERS, LANES), f32),
            dma((BLOCKS,)),
            dma((STEPS, 3)),
            dma((2,)),
            dma((STEPS, 2)),
            dma((CHUNKS + 1,)),
            dma((STEPS, 2, CHUNKS)),
            dma((STEPS, 2, CHUNKS)),
            dma((STEPS, 2, CHUNKS)),
            dma((STEPS, 2, CHUNKS)),
            dma((STEPS,)),
            dma((STEPS, CHUNKS)),
            dma((1,)),
            dma((CHUNKS,)),
            dma((STEPS, BLOCKS, 2)),
            dma((STEPS,)),
            dma((STEPS, 2)),
            dma((STEPS, 2)),
            dma((STEPS, 2)),
            dma((STEPS, 2)),
            dma((STEPS, 2)),
            dma((STEPS, 2)),
        ],
        compiler_params=pltpu.CompilerParams(
            collective_id=0, has_side_effects=True, vmem_limit_bytes=48 * 1024 * 1024
        ),
        cost_estimate=pl.CostEstimate(flops=35_000_000, bytes_accessed=11_000_000, transcendentals=0),
    )(*(pltpu.with_memory_space_constraint(a, pltpu.HBM) for a in (seed_fluid, seed_plate, velocity, enthalpy, phase, contact)))


def solution(mesh):
    return jax.shard_map(
        on_device,
        mesh=mesh,
        in_specs=(
            P("ty", "tx", None),
            P(None, "ty", "tx"),
            P(None, None, "ty", "tx", None),
            P(None, None, "ty", "tx"),
            P(None, None, "ty", "tx"),
            P("ty", "tx"),
        ),
        out_specs=(P("ty", "tx", None), P(None, "ty", "tx")),
        check_vma=False,
    )
```

time: 52.9 us -> 49.3 us (0.932)
  local copies, waits for them, and re-layouts: 7.01 us -> 1.67 us
  Pallas kernels: 44.9 us -> 46.8 us
    unnamed x12 -> x2, local copies, waits for them, and re-layouts: 7.01 us -> 1.67 us
    pallas_call x1, Pallas kernels: 44.9 us -> 46.8 us  [on_device(): pl.pallas_call(kernel, out_shape=(jax.ShapeDtypeStruct(seed_fluid.shape,...]
where the time goes in v2:
time: 49.3 us; the launch traced here: 49.2 us
  Pallas kernels  46.8 us (95%)
  local copies, waits for them, and re-layouts  1.67 us (3%)
  between operations  0.64 us (1%)
    pallas_call x1, Pallas kernels, on_device(): pl.pallas_call(kernel, out_shape=(jax.ShapeDtypeStruct(seed_fluid.shape,...  46.8 us
    unnamed x2, local copies, waits for them, and re-layouts  1.67 us

profile of v2, /device:TPU:6, one launch (start us, length us, event | category | flops | bytes accessed | tf_op | source)
XLA Modules:
  0.0 49.2 jit_solution(13533270156557835056)
XLA Ops:
  0.6 46.8 %shard_map.77 = (f32[4,64,1024]{2,1,0:T(8,128)S(1)}, f32[16,32,128]{2,1,0:T(8,128)S(1)}) custom-call(f32[4,64,1024]{2,1,0:T(8,128)} %seed_fluid.1, f32[16,32,128]{2,1,0:T(8,128)} %seed_plate.1, bf16[4,3,4,64,1024]{4,3,2,1,0:T(8,128)(2,1)} %velocity.1, f32[4,16,32,128]{3,2,1,0:T(8,128)} %enthalpy.1, s32[4,16,32,128]{3,2,1,0:T(8,128)} %phase.1, s32[32,128]{1,0:T(8,128)} %contact.1), custom_call_target="tpu_custom_call" | custom-call | flops 35000000 | bytes 11000000 | tf_op jit(solution)/shard_map/pallas_call | solution.py:620
  47.5 1.0 %copy.10 = f32[4,64,1024]{2,1,0:T(8,128)} copy(f32[4,64,1024]{2,1,0:T(8,128)S(1)} %get-tuple-element.4) | data formatting | bytes 2097152
  48.5 0.7 %copy.11 = f32[16,32,128]{2,1,0:T(8,128)} copy(f32[16,32,128]{2,1,0:T(8,128)S(1)} %get-tuple-element.5) | data formatting | bytes 524288

commit v3 on v2

--- a/solution.py
+++ b/solution.py
@@ -14,9 +14,14 @@
 CHUNKS = 4
 PROWS = 32
 LANES = 128
-PLATE_SLOTS = ((0, 5), (1, 8), (2, 11), (3, 15))
-CARRY_SLOTS = ((1, 8), (2, 12), (3, 15))
-COUPLE_SLOTS = ((0, 5), (1, 10), (2, 12), (3, 15))
+STEP_SLOTS = ((0, 1), (1, 6), (2, 9), (3, 14))
+TOP_SLOTS = ((0, 4), (1, 6), (2, 12), (3, 15))
+CARRY_SLOTS = ((1, 8), (2, 11), (3, 15))
+COUPLE_SLOTS = ((0, 4), (1, 8), (2, 12), (3, 15))
+TOP_0, BASE_1, TOP_2, BASE_3, CONTACT, SLOPE_1, SLOPE_3 = range(7)
+PLANES = 7
+PASS_SLOTS = ((TOP_0, 1), (BASE_1, 4), (TOP_2, 10), (BASE_3, 13))
+MORE_PASS_SLOTS = ((CONTACT, 1), (SLOPE_1, 2), (SLOPE_3, 11))
 TX = 8
 TY = 16
 
@@ -24,10 +29,10 @@
 def kernel(
     seed_fluid, seed_plate, velocity, enthalpy, phase, contact,
     out_fluid, out_plate,
-    F, NF, V, ZS, ZR, YS, YR, CR, CC, CF, CI, PR, PT, NP, TOP, EN, PH, SL, PYS, PYR, PXS, PXR, SXM, SXP, AS, AM, CP, D, ND, DXM, DXP, DYS, DYR,
+    F, NF, V, ZS, ZR, YS, YR, CR, RB, KP, CI, PR, PT, NP, TOP, EN, PH, SL, PYS, PYR, PXS, PXR, SXM, SXP, AS, AM, WD, CP, D, ND, DXM, DXP, DYS, DYR,
     load_f, load_v, load_p, load_e, out_sem,
-    zs_sem, zr_sem, ys_sem, yr_sem, cs_sem, cr_sem, ccs_sem, ccr_sem, fs_sem, pr_sem,
-    pys_sem, pyr_sem, pxs_sem, pxr_sem, dys_sem, dyr_sem,
+    zs_sem, zr_sem, ys_sem, yr_sem, cs_sem, rb_sem, fw_sem, cr_sem, fs_sem, pr_sem,
+    pys_sem, pyr_sem, pxs_sem, pxr_sem, dys_sem, dyr_sem, present,
 ):
     tx = lax.axis_index("tx")
     ty = lax.axis_index("ty")
@@ -36,7 +41,11 @@
     is_wall = ty == 0
     home_tx = ty // 2
     is_self = (tx == 0) & (ty == 0)
-    not_self = jnp.logical_not(is_self)
+    parity, core = lax.rem(ty // 2, 2), lax.rem(ty, 2)
+    pass_tx = 2 * (tx // 2) + parity
+    away_from_pass = (pass_tx != tx) | (ty != 1)
+    is_pass = ty == 1
+    column, high = tx // 2, lax.rem(tx, 2)
     lane = lax.broadcasted_iota(jnp.int32, (ROWS, LANES), 1)
     row = lax.broadcasted_iota(jnp.int32, (ROWS, LANES), 0)
 
@@ -71,19 +80,33 @@
 
         return jnp.where(cond, 1, 0)
 
-    expected = greet(not_self, (home_tx, 0))
-    expected += greet(has_lo, (tx - 1, ty))
-    expected += greet(has_hi, (tx + 1, ty))
-    expected += greet(has_down, (tx, ty - 1))
-    expected += greet(has_up, (tx, ty + 1))
-
     @pl.when(is_wall)
     def _():
         for c in range(TX):
             for r in range(2):
                 greet((tx > 0) | (2 * c + r > 0), (c, 2 * tx + r))
 
-    expected += jnp.where(is_wall, jnp.where(is_self, 15, 16), 0)
+    expected = jnp.where(is_self, 0, 1)
+
+    @pl.when(is_pass)
+    def _():
+        for z in range(4):
+            for k in range(4):
+                to = (2 * column + k // 2, 4 * z + 2 * high + k % 2)
+                greet((to[0] != tx) | (to[1] != ty), to)
+
+    expected += jnp.where(away_from_pass, 1, 0)
+
+    @pl.when(is_wall)
+    def _():
+        for x in range(4):
+            greet(is_wall, (2 * x + high, 1))
+
+    expected += jnp.where(is_pass, 4, 0)
+    expected += greet(has_lo, (tx - 1, ty))
+    expected += greet(has_hi, (tx + 1, ty))
+    expected += greet(has_down, (tx, ty - 1))
+    expected += greet(has_up, (tx, ty + 1))
 
     for n in (3, 2, 1, 0):
         e, p, v = late_loads(n)
@@ -100,22 +123,22 @@
 
     def z_down(s, j):
         blocks = pl.ds(2 * j, 2)
-        return remote(ZS.at[s, 0, blocks], ZR.at[s, 1, blocks], zs_sem.at[s, 0, j], zr_sem.at[s, 1, j], (tx, ty - 1))
+        return remote(ZS.at[s, 0, blocks], ZR.at[s, 1, blocks], zs_sem.at[0], zr_sem.at[s, 1, j], (tx, ty - 1))
 
     def z_up(s, j):
         blocks = pl.ds(2 * j, 2)
-        return remote(ZS.at[s, 1, blocks], ZR.at[s, 0, blocks], zs_sem.at[s, 1, j], zr_sem.at[s, 0, j], (tx, ty + 1))
+        return remote(ZS.at[s, 1, blocks], ZR.at[s, 0, blocks], zs_sem.at[1], zr_sem.at[s, 0, j], (tx, ty + 1))
 
     def y_lo(s, j):
-        return remote(YS.at[s, 0, j], YR.at[s, 1, j], ys_sem.at[s, 0, j], yr_sem.at[s, 1, j], (tx - 1, ty))
+        return remote(YS.at[s, 0, j], YR.at[s, 1, j], ys_sem.at[0], yr_sem.at[s, 1, j], (tx - 1, ty))
 
     def y_hi(s, j):
-        return remote(YS.at[s, 1, j], YR.at[s, 0, j], ys_sem.at[s, 1, j], yr_sem.at[s, 0, j], (tx + 1, ty))
+        return remote(YS.at[s, 1, j], YR.at[s, 0, j], ys_sem.at[1], yr_sem.at[s, 0, j], (tx + 1, ty))
 
     def wall_out(s, j, bb, r):
         b = 2 * j + bb
         return remote(
-            AM.at[s, b, pl.ds(PROWS * r, PROWS)], PR.at[s], fs_sem.at[s, b, r], pr_sem.at[s], (b, 2 * tx + r)
+            AM.at[s, b, pl.ds(PROWS * r, PROWS)], PR.at[s], fs_sem.at[s], pr_sem.at[s], (b, 2 * tx + r)
         )
 
     def each_wall_out(s, j, act):
@@ -141,12 +164,6 @@
         @pl.when(is_self & (j == 0))
         def _():
             pltpu.make_async_copy(AM.at[s, 0, pl.ds(0, PROWS)], PR.at[s], pr_sem.at[s]).start()
-
-    def sent(s, j):
-        pl.when(has_lo)(lambda: y_lo(s, j).wait_send())
-        pl.when(has_hi)(lambda: y_hi(s, j).wait_send())
-        pl.when(has_down)(lambda: z_down(s, j).wait_send())
-        pl.when(has_up)(lambda: z_up(s, j).wait_send())
 
     def stage_z(s, j):
         n = STEPS - 1 - s
@@ -255,13 +272,12 @@
             def _():
                 for bb in range(2):
                     AM[1, 2 * j + bb] = NF[2 * j + bb, 0]
-                wall_launch(1, j)
 
     def d_lo(s):
-        return remote(DYS.at[s, 0], DYR.at[s, 1], dys_sem.at[s, 0], dyr_sem.at[s, 1], (tx - 1, ty))
+        return remote(DYS.at[s, 0], DYR.at[s, 1], dys_sem.at[0], dyr_sem.at[s, 1], (tx - 1, ty))
 
     def d_hi(s):
-        return remote(DYS.at[s, 1], DYR.at[s, 0], dys_sem.at[s, 1], dyr_sem.at[s, 0], (tx + 1, ty))
+        return remote(DYS.at[s, 1], DYR.at[s, 0], dys_sem.at[1], dyr_sem.at[s, 0], (tx + 1, ty))
 
     def carry_on(s):
         prime(s, D, DXP, DXM)
@@ -280,8 +296,16 @@
                         q = LAYERS * (b % 2) + l
                         ND[b, l, at : at + 1, :] += DYR[s, side, b // 2, q : q + 1, :]
 
-        pl.when(has_lo)(lambda: d_lo(s).wait_send())
-        pl.when(has_hi)(lambda: d_hi(s).wait_send())
+        @pl.when(s == STEPS - 1)
+        def _():
+            def body(b, c):
+                for l in range(LAYERS):
+                    F[b, l] += ND[b, l]
+                upper = pl.ds(1, LAYERS - 1)
+                pltpu.make_async_copy(F.at[b, upper], out_fluid.at[upper, :, lanes(b)], out_sem.at[b // 2]).start()
+                return c
+
+            lax.fori_loop(0, BLOCKS, body, 0)
 
         @pl.when(s < STEPS - 1)
         def _():
@@ -295,21 +319,53 @@
             lax.fori_loop(0, CHUNKS, body, 0)
 
     def couple(s):
-        for j in range(CHUNKS):
-            blocks = pl.ds(2 * j, 2)
-            pltpu.make_async_copy(CR.at[s, blocks], CR.at[s, blocks], cr_sem.at[s, j]).wait()
-
-        @pl.when(s == 0)
-        def _():
+        def here(p):
             for j in range(CHUNKS):
                 blocks = pl.ds(2 * j, 2)
-                pltpu.make_async_copy(CC.at[blocks], CC.at[blocks], ccr_sem.at[j]).wait()
+                pltpu.make_async_copy(CR.at[p, blocks], CR.at[p, blocks], cr_sem.at[p, j]).wait()
+
+        here(s)
+        odd = lax.rem(s, 2) == 1
+
+        @pl.when(s == 0)
+        def _():
+            here(CONTACT)
+
+        @pl.when(odd)
+        def _():
+            slope = SLOPE_1 + s // 2
+            here(slope)
+
+            def body(b, c):
+                KP[b] = CR[s, b] - CR[slope, b] * KP[b]
+                return c
+
+            lax.fori_loop(0, BLOCKS, body, 0)
+
+        @pl.when(jnp.logical_not(odd))
+        def _():
+            def body(b, c):
+                KP[b] = CR[s, b]
+                return c
+
+            lax.fori_loop(0, BLOCKS, body, 0)
 
         def body(b, c):
             wall = AS[s, b] + D[b, 0]
-            D[b, 0] = ND[b, 0] + CC[b] * (0.5 * CR[s, b] - 0.5 * wall)
-            for l in range(1, LAYERS):
-                D[b, l] = ND[b, l]
+            coupling = CR[CONTACT, b] * (0.5 * KP[b] - 0.5 * wall)
+            KP[b] = coupling
+
+            @pl.when(s < STEPS - 1)
+            def _():
+                D[b, 0] = ND[b, 0] + coupling
+                for l in range(1, LAYERS):
+                    D[b, l] = ND[b, l]
+
+            @pl.when(s == STEPS - 1)
+            def _():
+                F[b, 0] += coupling
+                pltpu.make_async_copy(F.at[b, 0:1], out_fluid.at[0:1, :, lanes(b)], out_sem.at[b // 2]).start()
+
             return c
 
         lax.fori_loop(0, BLOCKS, body, 0)
@@ -323,63 +379,52 @@
             lax.fori_loop(0, CHUNKS, body, 0)
             pl.when(has_lo)(lambda: d_lo(s + 1).start())
             pl.when(has_hi)(lambda: d_hi(s + 1).start())
-
-        @pl.when(s == STEPS - 1)
-        def _():
-            def body(b, c):
-                for l in range(LAYERS):
-                    F[b, l] += D[b, l]
-                return c
-
-            lax.fori_loop(0, BLOCKS, body, 0)
-            for j in range(CHUNKS):
-                put_out(j)
 
     def put_out(j):
         for bb in range(2):
             b = 2 * j + bb
             pltpu.make_async_copy(F.at[b], out_fluid.at[:, :, lanes(b)], out_sem.at[j]).start()
 
-    tile_rows = pl.ds(pl.multiple_of(PROWS * lax.rem(ty, 2), PROWS), PROWS)
-    tile_chunk = tx // 2
-
-    def wall_in(s):
-        return remote(TOP.at[s], CR.at[s, tx, tile_rows], cs_sem.at[s], cr_sem.at[s, tile_chunk], (home_tx, 0))
-
-    def contact_in():
-        return remote(CF, CC.at[tx, tile_rows], ccs_sem.at[0], ccr_sem.at[tile_chunk], (home_tx, 0))
+
+    def reply(p):
+        return remote(TOP.at[p], RB.at[p, ty // 4, high, core_rows], cs_sem.at[0], rb_sem.at[p], (pass_tx, 1))
+
+    def passed(p, z):
+        return remote(
+            RB.at[p, z], CR.at[p, pl.ds(2 * column, 2)], fw_sem.at[p], cr_sem.at[p, column], (2 * z + high, 0)
+        )
+
+    core_rows = pl.ds(pl.multiple_of(PROWS * core, PROWS), PROWS)
+
+    def wall_reply(p):
+        pl.when(away_from_pass)(lambda: reply(p).start())
+
+        @pl.when(jnp.logical_not(away_from_pass))
+        def _():
+            pltpu.make_async_copy(TOP.at[p], RB.at[p, ty // 4, high, core_rows], rb_sem.at[p]).start()
+
+    def pass_on(p):
+        pltpu.make_async_copy(RB.at[p], RB.at[p], rb_sem.at[p]).wait()
+        for z in range(4):
+            passed(p, z).start()
 
     def py_lo(s):
-        return remote(PYS.at[s, 0], PYR.at[s, 1], pys_sem.at[s, 0], pyr_sem.at[s, 1], (tx, ty - 1))
+        return remote(PYS.at[s, 0], PYR.at[s, 1], pys_sem.at[0], pyr_sem.at[s, 1], (tx, ty - 1))
 
     def py_hi(s):
-        return remote(PYS.at[s, 1], PYR.at[s, 0], pys_sem.at[s, 1], pyr_sem.at[s, 0], (tx, ty + 1))
+        return remote(PYS.at[s, 1], PYR.at[s, 0], pys_sem.at[1], pyr_sem.at[s, 0], (tx, ty + 1))
 
     def px_lo(s):
-        return remote(PXS.at[s], PXR.at[s, 1], pxs_sem.at[s, 0], pxr_sem.at[s, 1], (tx - 1, ty))
+        return remote(PXS.at[s], PXR.at[s, 1], pxs_sem.at[0], pxr_sem.at[s, 1], (tx - 1, ty))
 
     def px_hi(s):
-        return remote(PXS.at[s], PXR.at[s, 0], pxs_sem.at[s, 1], pxr_sem.at[s, 0], (tx + 1, ty))
-
-    def wall_reply(s):
-        pl.when(not_self)(lambda: wall_in(s).start())
-
-        @pl.when(is_self)
-        def _():
-            pltpu.make_async_copy(TOP.at[s], CR.at[s, 0, pl.ds(0, PROWS)], cr_sem.at[s, 0]).start()
+        return remote(PXS.at[s], PXR.at[s, 0], pxs_sem.at[1], pxr_sem.at[s, 0], (tx + 1, ty))
 
     def plate_launch(s):
         pl.when(has_lo)(lambda: px_lo(s).start())
         pl.when(has_hi)(lambda: px_hi(s).start())
         pl.when(has_down)(lambda: py_lo(s).start())
         pl.when(has_up)(lambda: py_hi(s).start())
-
-    def plate_sent(s):
-        pl.when(not_self)(lambda: wall_in(s).wait_send())
-        pl.when(has_lo)(lambda: px_lo(s).wait_send())
-        pl.when(has_hi)(lambda: px_hi(s).wait_send())
-        pl.when(has_down)(lambda: py_lo(s).wait_send())
-        pl.when(has_up)(lambda: py_hi(s).wait_send())
 
     small_lane = lax.broadcasted_iota(jnp.int32, (8, LANES), 1)
 
@@ -446,26 +491,37 @@
                 total += PT[z + 1]
             NP[z] = value + SL[z] * (0.12 * (total - 6.0 * value))
 
+        @pl.when(lax.rem(s, 2) == 0)
+        def _():
+            TOP[s + 1] = NP[PZ - 1]
+            wall_reply(s + 1)
+
     def plate_top(s):
         pltpu.make_async_copy(PR.at[s], PR.at[s], pr_sem.at[s]).wait()
         wall = PR[s] + jnp.where(s > 0, CP[...], 0.0)
-        coupling = CF[...] * (0.5 * PT[PZ - 1] - 0.5 * wall)
+        coupling = TOP[CONTACT] * (0.5 * PT[PZ - 1] - 0.5 * wall)
         CP[...] = coupling
         value = NP[PZ - 1] - SL[PZ - 1] * coupling
         NP[PZ - 1] = value
 
         @pl.when(s < STEPS - 1)
         def _():
-            TOP[s + 1] = value
-            wall_reply(s + 1)
+            @pl.when(s == 1)
+            def _():
+                TOP[TOP_2] = value
+                wall_reply(TOP_2)
+
             plate_edges(s + 1, NP)
             plate_launch(s + 1)
 
-        plate_sent(s)
-
         @pl.when(s < STEPS - 1)
         def _():
             slopes_of(STEPS - 2 - s)
+
+            @pl.when(s == 1)
+            def _():
+                TOP[SLOPE_3] = SL[PZ - 1]
+                wall_reply(SLOPE_3)
 
         @pl.when(s == STEPS - 1)
         def _():
@@ -484,7 +540,7 @@
                 PXR[s, side] = jnp.zeros((8, LANES), jnp.float32)
 
     contact_load.wait()
-    CF[...] = CI[...].astype(jnp.float32)
+    TOP[CONTACT] = CI[...].astype(jnp.float32)
     for copy in f_loads:
         copy.wait()
     for c in (2, 1, 0):
@@ -507,29 +563,16 @@
                 ND[b, l] = jnp.zeros((ROWS, LANES), jnp.float32)
 
     plate_load.wait()
-    TOP[0] = PT[PZ - 1]
+    TOP[TOP_0] = PT[PZ - 1]
     plate_edges(0, PT)
     pl.semaphore_wait(barrier, expected)
 
-    def first_wall(chunk):
-        @pl.when(tile_chunk == chunk)
-        def _():
-            wall_reply(0)
-            pl.when(not_self)(lambda: contact_in().start())
-
-            @pl.when(is_self)
-            def _():
-                pltpu.make_async_copy(CF, CC.at[0, pl.ds(0, PROWS)], ccr_sem.at[0]).start()
-
-    first_wall(0)
-
-    @pl.when(is_wall)
+    @pl.when(jnp.logical_not(is_self))
     def _():
-        def body(j, carry):
-            wall_launch(0, j)
-            return carry
-
-        lax.fori_loop(0, CHUNKS, body, 0)
+        pl.semaphore_signal(present, inc=1, device_id=(home_tx, 0), device_id_type=MESH)
+
+    wall_reply(CONTACT)
+    wall_reply(TOP_0)
 
     def first_launch(j, carry):
         launch_y(0, j)
@@ -537,7 +580,6 @@
         return carry
 
     lax.fori_loop(0, CHUNKS, first_launch, 0)
-    first_wall(1)
     plate_launch(0)
 
     def first_interior(b, carry):
@@ -546,10 +588,10 @@
 
     prime(0, F, SXP, SXM)
     lax.fori_loop(0, BLOCKS // 2, first_interior, 0)
-    first_wall(2)
     lax.fori_loop(BLOCKS // 2, BLOCKS, first_interior, 0)
-    first_wall(3)
     slopes_of(STEPS - 1)
+    TOP[SLOPE_1] = SL[PZ - 1]
+    wall_reply(SLOPE_1)
 
     def at(t, slots, act):
         due, s = False, 0
@@ -557,10 +599,6 @@
             due, s = due | (t == place), jnp.where(t == place, step, s)
         pl.when(due)(lambda: act(s))
 
-    def plate(s):
-        plate_step(s)
-        plate_top(s)
-
     def slot(t, carry):
         s, j = t // CHUNKS, lax.rem(t, CHUNKS)
         finish(s, j)
@@ -588,27 +626,65 @@
             lax.fori_loop(jnp.maximum(2 * j - 1, 0), jnp.where(j == CHUNKS - 1, BLOCKS, 2 * j + 1), body, 0)
 
         pl.when((s == STEPS - 1) & (ty > 0))(lambda: put_out(j))
-        sent(s, j)
+
+        @pl.when(is_pass)
+        def _():
+            at(t, MORE_PASS_SLOTS, pass_on)
+            at(t, PASS_SLOTS, pass_on)
+
+        @pl.when(is_wall & (t == 0))
+        def _():
+            pl.semaphore_wait(present, jnp.where(tx == 0, 15, 16))
+
+            def body(j, c):
+                wall_launch(0, j)
+                return c
+
+            lax.fori_loop(0, CHUNKS, body, 0)
+
+        pl.when(is_wall & (s == 0))(lambda: wall_launch(1, j))
 
         @pl.when(is_wall)
         def _():
             at(t, CARRY_SLOTS, carry_on)
             at(t, COUPLE_SLOTS, couple)
 
-        at(t, PLATE_SLOTS, plate)
+        at(t, STEP_SLOTS, plate_step)
+        at(t, TOP_SLOTS, plate_top)
         return carry
 
     lax.fori_loop(0, STEPS * CHUNKS, slot, 0)
+
+    def all_sent(ref, semaphore):
+        pltpu.make_async_copy(ref, ref, semaphore).wait()
+
+    pl.when(away_from_pass)(lambda: all_sent(TOP, cs_sem.at[0]))
+    some = pl.ds(0, STEPS)
+    for there, k, z_or_y, z_or_y_sem, plate, plate_sem in (
+        (has_lo, 0, YS.at[:, 0], ys_sem, PXS.at[some], pxs_sem),
+        (has_hi, 1, YS.at[:, 1], ys_sem, PXS.at[some], pxs_sem),
+        (has_down, 0, ZS.at[:, 0], zs_sem, PYS.at[some, 0], pys_sem),
+        (has_up, 1, ZS.at[:, 1], zs_sem, PYS.at[some, 1], pys_sem),
+    ):
+        @pl.when(there)
+        def _(k=k, z_or_y=z_or_y, z_or_y_sem=z_or_y_sem, plate=plate, plate_sem=plate_sem):
+            all_sent(z_or_y, z_or_y_sem.at[k])
+            all_sent(plate, plate_sem.at[k])
+
+    for there, k in ((has_lo, 0), (has_hi, 1)):
+        pl.when(is_wall & there)(lambda k=k: all_sent(DYS.at[pl.ds(1, STEPS - 1), k], dys_sem.at[k]))
+
+    @pl.when(is_pass)
+    def _():
+        for p in range(PLANES):
+            all_sent(RB.at[p], fw_sem.at[p])
 
     @pl.when(is_wall)
     def _():
-        def body(t, c):
-            each_wall_out(t // CHUNKS, lax.rem(t, CHUNKS), lambda copy: copy.wait_send())
-            return c
-
-        lax.fori_loop(0, STEPS * CHUNKS, body, 0)
-
-    pl.when(not_self)(lambda: contact_in().wait_send())
+        for s in range(STEPS):
+            pl.when(is_self)(lambda s=s: all_sent(WD, fs_sem.at[s]))
+            pl.when(jnp.logical_not(is_self))(lambda s=s: all_sent(AM.at[s], fs_sem.at[s]))
+
     for j in range(CHUNKS):
         pltpu.make_async_copy(F.at[pl.ds(2 * j, 2)], F.at[pl.ds(2 * j, 2)], out_sem.at[j]).wait()
     pltpu.make_async_copy(NP, out_plate, out_sem.at[CHUNKS]).wait()
@@ -633,14 +709,14 @@
             pltpu.VMEM((STEPS, 2, BLOCKS, ROWS, LANES), f32),
             pltpu.VMEM((STEPS, 2, CHUNKS, 2 * LAYERS, LANES), f32),
             pltpu.VMEM((STEPS, 2, CHUNKS, 2 * LAYERS, LANES), f32),
-            pltpu.VMEM((STEPS, BLOCKS, ROWS, LANES), f32),
+            pltpu.VMEM((PLANES, BLOCKS, ROWS, LANES), f32),
+            pltpu.VMEM((PLANES, 4, 2, ROWS, LANES), f32),
             pltpu.VMEM((BLOCKS, ROWS, LANES), f32),
-            pltpu.VMEM((PROWS, LANES), f32),
             pltpu.VMEM((PROWS, LANES), jnp.int32),
             pltpu.VMEM((STEPS, PROWS, LANES), f32),
             pltpu.VMEM((PZ, PROWS, LANES), f32),
             pltpu.VMEM((PZ, PROWS, LANES), f32),
-            pltpu.VMEM((STEPS, PROWS, LANES), f32),
+            pltpu.VMEM((PLANES, PROWS, LANES), f32),
             pltpu.VMEM((STEPS, PZ, PROWS, LANES), f32),
             pltpu.VMEM((STEPS, PZ, PROWS, LANES), jnp.int32),
             pltpu.VMEM((PZ, PROWS, LANES), f32),
@@ -652,6 +728,7 @@
             pltpu.VMEM((LAYERS, ROWS, LANES), f32),
             pltpu.VMEM((STEPS, BLOCKS, ROWS, LANES), f32),
             pltpu.VMEM((STEPS, BLOCKS, ROWS, LANES), f32),
+            pltpu.VMEM((2 * TX - 1, PROWS, LANES), f32),
             pltpu.VMEM((PROWS, LANES), f32),
             pltpu.VMEM((BLOCKS, LAYERS, ROWS, LANES), f32),
             pltpu.VMEM((BLOCKS, LAYERS, ROWS, LANES), f32),
@@ -664,22 +741,23 @@
             dma((2,)),
             dma((STEPS, 2)),
             dma((CHUNKS + 1,)),
+            dma((2,)),
             dma((STEPS, 2, CHUNKS)),
+            dma((2,)),
             dma((STEPS, 2, CHUNKS)),
-            dma((STEPS, 2, CHUNKS)),
-            dma((STEPS, 2, CHUNKS)),
+            dma((1,)),
+            dma((PLANES,)),
+            dma((PLANES,)),
+            dma((PLANES, CHUNKS)),
             dma((STEPS,)),
-            dma((STEPS, CHUNKS)),
-            dma((1,)),
-            dma((CHUNKS,)),
-            dma((STEPS, BLOCKS, 2)),
             dma((STEPS,)),
+            dma((2,)),
             dma((STEPS, 2)),
+            dma((2,)),
             dma((STEPS, 2)),
+            dma((2,)),
             dma((STEPS, 2)),
-            dma((STEPS, 2)),
-            dma((STEPS, 2)),
-            dma((STEPS, 2)),
+            pltpu.SemaphoreType.REGULAR,
         ],
         compiler_params=pltpu.CompilerParams(
             collective_id=0, has_side_effects=True, vmem_limit_bytes=48 * 1024 * 1024

time: 49.3 us -> 45.4 us (0.921); the launches traced: 49.2 us -> 44.5 us
  Pallas kernels: 46.8 us -> 42.2 us
    pallas_call x1, Pallas kernels: 46.8 us -> 42.2 us  [on_device(): pl.pallas_call(kernel, out_shape=(jax.ShapeDtypeStruct(seed_fluid.shape,...]
where the time goes in v3:
time: 45.4 us; the launch traced here: 44.5 us
  Pallas kernels  42.2 us (93%)
  local copies, waits for them, and re-layouts  1.67 us (4%)
  between operations  0.64 us (1%)
    pallas_call x1, Pallas kernels, on_device(): pl.pallas_call(kernel, out_shape=(jax.ShapeDtypeStruct(seed_fluid.shape,...  42.2 us
    unnamed x2, local copies, waits for them, and re-layouts  1.67 us

profile of v3, /device:TPU:6, one launch (start us, length us, event | category | flops | bytes accessed | tf_op | source)
XLA Modules:
  0.0 44.5 jit_solution(5975254049034993239)
XLA Ops:
  0.6 42.2 %shard_map.77 = (f32[4,64,1024]{2,1,0:T(8,128)S(1)}, f32[16,32,128]{2,1,0:T(8,128)S(1)}) custom-call(f32[4,64,1024]{2,1,0:T(8,128)} %seed_fluid.1, f32[16,32,128]{2,1,0:T(8,128)} %seed_plate.1, bf16[4,3,4,64,1024]{4,3,2,1,0:T(8,128)(2,1)} %velocity.1, f32[4,16,32,128]{3,2,1,0:T(8,128)} %enthalpy.1, s32[4,16,32,128]{3,2,1,0:T(8,128)} %phase.1, s32[32,128]{1,0:T(8,128)} %contact.1), custom_call_target="tpu_custom_call" | custom-call | flops 35000000 | bytes 11000000 | tf_op jit(solution)/shard_map/pallas_call | solution.py:696
  42.8 1.0 %copy.10 = f32[4,64,1024]{2,1,0:T(8,128)} copy(f32[4,64,1024]{2,1,0:T(8,128)S(1)} %get-tuple-element.4) | data formatting | bytes 2097152
  43.8 0.7 %copy.11 = f32[16,32,128]{2,1,0:T(8,128)} copy(f32[16,32,128]{2,1,0:T(8,128)S(1)} %get-tuple-element.5) | data formatting | bytes 524288
